TPU v7x, 32 devices: a whole 2x2x4 slice. The times are simulated.
32 devices in a mesh: px: 4 (over y, core), py: 8 (over z, x).
Axes of the slice: x: 2, y: 2, z: 4, core: 2. Of those that a mesh axis runs over, the one named last changes fastest.
Arguments:
- fine_residual: bfloat16 [131072, 256], P(('px', 'py')), may hold values from -6 to 6
- dest_owner: int32 [131072], P(('px', 'py')), may hold values from 0 to 31, as said below
- coarse_slot: int32 [131072], P(('px', 'py')), may hold values from 0 to 511, as said below
- ghost_slot: int32 [128, 32], P(('px', 'py')), may hold values from 0 to 511, as said below
- child_type: int32 [131072], P(('px', 'py')), may hold values from 0 to 7
- restrict_table: bfloat16 [8, 64, 64], replicated, may hold values from -0.75 to 0.75
- inverse_blocks: bfloat16 [16384, 4096], P(('px', 'py')), may hold values from -0.45 to 1.05
- face_table: bfloat16 [6, 64, 64], replicated, may hold values from -0.75 to 0.75
- face_coef: float32 [16], replicated, may hold values from 0.2 to 2
- coef_index: int32 [6, 16384], P(None, ('px', 'py')), may hold values from 0 to 15
- neighbours: int32 [6, 16384], P(None, ('px', 'py')), may hold values from 0 to 16383, as said below
Outputs:
- coarse_solution: float32 [16384, 256], P(('px', 'py'))
- fine_correction: bfloat16 [131072, 256], P(('px', 'py'))
Inputs may be any that keep to these rules, and one draw needn't show every extreme that they name: `dest_owner`: the owner is the element's own device or a device one step away along py (same px index) or along px (same py index); every coarse element has exactly 8 fine children, with distinct child_type. `coarse_slot`: for an element whose parent lives on another device the value is below 32. `ghost_slot`: j = 0, 1, 2, 3 stands for the device one lower along py, one higher along py, one lower along px, one higher along px; a device's four lists hold distinct elements; each remote child of a device's coarse element is found in the list toward the child's device, at the row that its coarse_slot names; between two neighbouring devices at most 32 parents have children across, and some pair has exactly 32. `neighbours`: the element across a face lives on the same device or on a device one step away along py or along px, never outside the grid.
All inputs are finite; a program needn't handle non-finite values.
Results may differ from a plain program's by a relative error of at most 0.0073.
Values may be sent and summed in bfloat16 or wider, within the bound.
A program may use at most 64 MiB of HBM per device.

v0:
```python
import math

import jax
import jax.numpy as jnp
from jax import lax
from jax.sharding import PartitionSpec as P

omega = 0.5


def padded(cells, sides, width):
    for axis, dim in sides:
        count = lax.axis_size(axis)
        ends = count - 1
        head = lax.slice_in_dim(cells, 0, width, axis=dim)
        tail = lax.slice_in_dim(cells, cells.shape[dim] - width, cells.shape[dim], axis=dim)
        cells = jnp.concatenate(
            [
                lax.ppermute(tail, axis, [(i, (i + 1) % count) for i in range(ends)]),
                cells,
                lax.ppermute(head, axis, [((i + 1) % count, i) for i in range(ends)]),
            ],
            axis=dim,
        )
    return cells


def stacked_table(matrices, flipped):
    order_dim = matrices.shape[1]
    if flipped:
        arranged = jnp.transpose(matrices, (1, 0, 2))
    else:
        arranged = jnp.transpose(matrices, (2, 0, 1))
    return arranged.reshape(order_dim, matrices.shape[0] * order_dim)


def typed_product(blocks, child_type, matrices, flipped):
    item_count = blocks.shape[0]
    row_width = blocks.shape[1]
    order_dim = matrices.shape[1]
    kind_count = matrices.shape[0]
    columns = blocks.reshape(item_count * (row_width // order_dim), order_dim)
    products = jnp.dot(
        columns, stacked_table(matrices, flipped), preferred_element_type=jnp.float32
    )
    products = products.reshape(item_count, row_width // order_dim, kind_count, order_dim)
    selector = (child_type[:, None] == jnp.arange(kind_count, dtype=jnp.int32)[None, :]).astype(
        jnp.float32
    )
    picked = jnp.sum(products * selector[:, None, :, None], axis=2)
    return picked.reshape(item_count, row_width)


def pick_rows(table, index):
    count = index.shape[0]
    table_rows = table.shape[0]
    block = math.gcd(count, 1024)

    def one_block(block_index):
        onehot = (block_index[:, None] == jnp.arange(table_rows, dtype=jnp.int32)[None, :]).astype(
            jnp.bfloat16
        )
        return jnp.dot(onehot, table, preferred_element_type=jnp.float32).astype(table.dtype)

    picked = lax.map(one_block, index.reshape(count // block, block))
    return picked.reshape(count, table.shape[1])


def compact_blocks(extended, coarse_count, row_width):
    return jnp.stack(
        [extended[0, 1], extended[1, 0], extended[1, 1], extended[1, 2], extended[2, 1]]
    ).reshape(5 * coarse_count, row_width)


def compact_number(block_number):
    return jnp.where(
        block_number == 1,
        0,
        jnp.where(
            block_number == 3,
            1,
            jnp.where(block_number == 4, 2, jnp.where(block_number == 5, 3, 4)),
        ),
    ).astype(jnp.int32)


def pack_joint(lists):
    return jnp.stack([jnp.stack([lists[2], lists[1]]), jnp.stack([lists[0], lists[3]])])


def unpack_joint(extended):
    return jnp.stack([extended[1, 0], extended[2, 3], extended[0, 2], extended[3, 1]])


def shards(
    fine_residual,
    dest_owner,
    coarse_slot,
    ghost_slot,
    child_type,
    restrict_table,
    inverse_blocks,
    face_table,
    face_coef,
    coef_index,
    neighbours,
):
    fine_count, row_width = fine_residual.shape
    coarse_count = inverse_blocks.shape[0]
    ghost_rows = ghost_slot.shape[1]
    order_dim = restrict_table.shape[1]
    rhs_count = row_width // order_dim
    width_py = lax.axis_size("py")
    index_px = lax.axis_index("px")
    index_py = lax.axis_index("py")
    own_index = index_px * width_py + index_py
    contrib = typed_product(fine_residual, child_type, restrict_table, False).astype(jnp.bfloat16)
    offset = dest_owner - own_index
    is_local = offset == 0
    direction = jnp.where(
        offset == -1, 0, jnp.where(offset == 1, 1, jnp.where(offset < 0, 2, 3))
    ).astype(jnp.int32)
    slot_onehot = (
        (coarse_slot[:, None] == jnp.arange(coarse_count, dtype=jnp.int32)[None, :])
        & is_local[:, None]
    ).astype(jnp.bfloat16)
    coarse_local = lax.dot_general(
        slot_onehot, contrib, (((0,), (0,)), ((), ())), preferred_element_type=jnp.float32
    )
    ghost_target = jnp.where(is_local, 4 * ghost_rows, direction * ghost_rows + coarse_slot)
    target_onehot = (
        ghost_target[:, None] == jnp.arange(4 * ghost_rows, dtype=jnp.int32)[None, :]
    ).astype(jnp.bfloat16)
    outgoing = lax.dot_general(
        target_onehot, contrib, (((0,), (0,)), ((), ())), preferred_element_type=jnp.float32
    )
    outgoing = outgoing.reshape(4, ghost_rows, row_width)
    along_py = padded(outgoing[0:2], (("py", 0),), 1)
    along_px = padded(outgoing[2:4], (("px", 0),), 1)
    incoming = jnp.stack([along_py[0], along_py[3], along_px[0], along_px[3]])
    list_onehot = (
        ghost_slot.reshape(-1)[:, None] == jnp.arange(coarse_count, dtype=jnp.int32)[None, :]
    ).astype(jnp.float32)
    arrived = lax.dot_general(
        list_onehot,
        incoming.reshape(4 * ghost_rows, row_width),
        (((0,), (0,)), ((), ())),
        precision=lax.Precision.HIGHEST,
        preferred_element_type=jnp.float32,
    )
    coarse_rhs = (coarse_local + arrived).astype(jnp.bfloat16)
    inverse = inverse_blocks.reshape(coarse_count, order_dim, order_dim)
    first_sweep = jnp.einsum(
        "cij,csj->csi",
        inverse,
        coarse_rhs.reshape(coarse_count, rhs_count, order_dim),
        preferred_element_type=jnp.float32,
    )
    first_sweep = first_sweep.reshape(coarse_count, row_width).astype(jnp.bfloat16)
    extended = padded(first_sweep.reshape(1, 1, coarse_count, row_width), (("px", 0), ("py", 1)), 1)
    nearby = compact_blocks(extended, coarse_count, row_width)
    across_owner = neighbours // coarse_count
    block_number = (across_owner // width_py - index_px + 1) * 3 + (
        across_owner % width_py - index_py + 1
    )
    local_index = compact_number(block_number) * coarse_count + neighbours % coarse_count
    beside = pick_rows(nearby, local_index.reshape(-1))
    faces_count = face_table.shape[0]
    kind_count = face_coef.shape[0]
    face_scale = jnp.sum(
        jnp.where(
            coef_index[:, :, None] == jnp.arange(kind_count, dtype=jnp.int32)[None, None, :],
            face_coef[None, None, :],
            jnp.float32(0.0),
        ),
        axis=2,
    )
    face_terms = jnp.einsum(
        "fcsj,fij->fcsi",
        beside.reshape(faces_count, coarse_count, rhs_count, order_dim),
        face_table,
        preferred_element_type=jnp.float32,
    )
    coupled = jnp.sum(face_terms * face_scale[:, :, None, None], axis=0).astype(jnp.bfloat16)
    correction = jnp.einsum(
        "cij,csj->csi", inverse, coupled, preferred_element_type=jnp.float32
    ).reshape(coarse_count, row_width)
    coarse_solution = first_sweep.astype(jnp.float32) - omega * correction
    answer = coarse_solution.astype(jnp.bfloat16)
    ghost_row = jnp.where(is_local, 0, coarse_slot)
    replies = pick_rows(answer, ghost_slot.reshape(-1)).reshape(4, ghost_rows, row_width)
    returned = unpack_joint(padded(pack_joint(replies), (("px", 0), ("py", 1)), 1))
    table = jnp.concatenate([returned.reshape(4 * ghost_rows, row_width), answer], axis=0)
    which = jnp.where(is_local, 4 * ghost_rows + coarse_slot, direction * ghost_rows + ghost_row)
    fetched = pick_rows(table, which)
    fine_correction = typed_product(fetched, child_type, restrict_table, True).astype(jnp.bfloat16)
    return (coarse_solution, fine_correction)


def solution(mesh):
    in_specs = (
        P(("px", "py"), None),
        P(("px", "py")),
        P(("px", "py")),
        P(("px", "py"), None),
        P(("px", "py")),
        P(),
        P(("px", "py"), None),
        P(),
        P(),
        P(None, ("px", "py")),
        P(None, ("px", "py")),
    )
    out_specs = (P(("px", "py"), None), P(("px", "py"), None))
    return jax.shard_map(shards, mesh=mesh, in_specs=in_specs, out_specs=out_specs, check_vma=False)
```

profile of v0, /device:TPU:0, one launch (start us, length us, event | category | flops | bytes accessed | tf_op | source)
XLA Modules:
  0.0 162.1 jit_solution(17929173991217031467)
XLA Ops:
  0.7 0.8 fusion.30
  1.5 3.0 %copy.88 = bf16[4096,256]{0,1:T(8,128)(2,1)S(1)} copy(bf16[4096,256]{1,0:T(8,128)(2,1)} %param.15) | data formatting | bytes 4194304 | tf_op args[0]
  4.5 5.5 %multiply_reduce_fusion.1 = bf16[4096,4,64]{0,2,1:T(8,128)(2,1)S(1)} fusion(f32[4096,8]{0,1:T(8,128)S(1)} %fusion.30, bf16[4096,4,64,1]{0,2,3,1:T(8,128)(2,1)S(1)} %bitcast.121, bf16[8,64,64]{2,1,0:T(8,128)(2,1)S(1)} %copy-done.3), kind=kOutput, calls=%fused_computation.15 | convolution fusion | flops 1089470464 | bytes 4390912 | tf_op jit(solution)/shard_map/dot_general | solution.py:43
  10.1 1.5 fusion.22
  11.6 4.8 %collective-permute-start = (f32[1,32,256]{2,1,0:T(8,128)S(1)}, f32[1,32,256]{2,1,0:T(8,128)S(1)}, u32[]{:S(2)}, u32[]{:S(2)}) collective-permute-start(f32[1,32,256]{2,1,0:T(8,128)S(1)} %get-tuple-element.108), channel_id=1, source_target_pairs={{0,1},{1,2},{2,3},{3,4},{4,5},{5,6},{6,7},{8,9},{9,10},{10,11},{11... | collective-permute-start | bytes 98312 | tf_op jit(solution)/shard_map/ppermute | solution.py:19
  16.4 1.3 collective-permute-start.1
  17.7 1.5 collective-permute-start.2
  19.2 1.3 collective-permute-start.3
  20.5 1.9 %fusion.11 = f32[512,256]{0,1:T(8,128)S(1)} fusion(bf16[4096,256]{0,1:T(8,128)(2,1)S(1)} %bitcast.133, s32[4096]{0:T(1024)S(1)} %copy-done.8, pred[4096]{0:T(1024)(128)(4,1)S(1)} %subtract_compare_fusion), kind=kOutput, calls=%fused_computation.18 | convolution fusion | flops 1077936128 | bytes 2641920 | tf_op jit(solution)/shard_map/dot_general | solution.py:127
  22.5 6.5 %copy.89 = bf16[512,4096]{0,1:T(8,128)(2,1)} copy(bf16[512,4096]{1,0:T(8,128)(2,1)} %param.21) | data formatting | bytes 8388608 | tf_op args[6]
  29.0 13.0 %copy.91 = bf16[512,64,64]{2,1,0:T(8,128)(2,1)} copy(bf16[512,64,64]{0,2,1:T(8,128)(2,1)} %bitcast.115) | data formatting | bytes 8388608 | tf_op jit(solution)/shard_map/reshape | solution.py:152
  42.0 0.5 fusion.21
  42.5 0.3 copy.90
  42.8 7.8 %fusion.45 = bf16[512,4,64]{2,1,0:T(4,128)(2,1)S(1)} fusion(bf16[512,4,64]{2,1,0:T(4,128)(2,1)S(1)} %copy.90, bf16[512,64,64]{2,1,0:T(8,128)(2,1)} %copy.91), kind=kOutput, calls=%fused_computation.98 | convolution fusion | flops 16777216 | bytes 4718592 | tf_op jit(solution)/shard_map/cij,csj->csi/dot_general | solution.py:153
  50.9 4.6 %collective-permute-start.4 = (bf16[1,1,512,256]{2,3,1,0:T(8,128)(2,1)S(1)}, bf16[1,1,512,256]{2,3,1,0:T(8,128)(2,1)S(1)}, u32[]{:S(2)}, u32[]{:S(2)}) collective-permute-start(bf16[1,1,512,256]{2,3,1,0:T(8,128)(2,1)S(1)} %bitcast.117), channel_id=1, source_target_pairs={{0,8},{8,16},{16,24},{1,9},{9,17},{17,25},{2,10},{10,18},{18,26},{... | collective-permute-start | bytes 786440 | tf_op jit(solution)/shard_map/ppermute | solution.py:19
  55.6 1.3 collective-permute-start.5
  56.9 3.3 %collective-permute-done.5 = bf16[1,1,512,256]{2,3,1,0:T(8,128)(2,1)S(1)} collective-permute-done((bf16[1,1,512,256]{2,3,1,0:T(8,128)(2,1)S(1)}, bf16[1,1,512,256]{2,3,1,0:T(8,128)(2,1)S(1)}, u32[]{:S(2)}, u32[]{:S(2)}) %collective-permute-start.5) | collective-permute-done | bytes 262176 | tf_op jit(solution)/shard_map/ppermute | solution.py:21
  60.3 5.5 %collective-permute-start.6 = (bf16[3,1,512,256]{2,3,1,0:T(8,128)(2,1)S(1)}, bf16[3,1,512,256]{2,3,1,0:T(8,128)(2,1)}, u32[]{:S(2)}, u32[]{:S(2)}) collective-permute-start(bf16[3,1,512,256]{2,3,1,0:T(8,128)(2,1)S(1)} %pad_maximum_fusion), channel_id=1, source_target_pairs={{0,1},{1,2},{2,3},{3,4},{4,5},{5,6},{6,7},{8,9},{9,10},{10,11},{11... | collective-permute-start | bytes 2359304 | tf_op jit(solution)/shard_map/ppermute | solution.py:19
  65.9 1.5 collective-permute-start.7
  67.6 28.2 %collective-permute-done.6 = bf16[3,1,512,256]{2,3,1,0:T(8,128)(2,1)} collective-permute-done((bf16[3,1,512,256]{2,3,1,0:T(8,128)(2,1)S(1)}, bf16[3,1,512,256]{2,3,1,0:T(8,128)(2,1)}, u32[]{:S(2)}, u32[]{:S(2)}) %collective-permute-start.6) | collective-permute-done | bytes 786464 | tf_op jit(solution)/shard_map/ppermute | solution.py:19
  95.8 1.0 fusion.26
  96.8 1.0 fusion.25
  97.8 0.6 copy.93
  98.4 8.0 %while.24 = (s32[]{:T(128)}, bf16[3,1024,256]{2,1,0:T(8,128)(2,1)}, s32[3,1024]{1,0:T(4,128)S(1)}, bf16[2560,256]{1,0:T(8,128)(2,1)S(1)}, s32[]{:T(128)}) while((s32[]{:T(128)}, bf16[3,1024,256]{2,1,0:T(8,128)(2,1)}, s32[3,1024]{1,0:T(4,128)S(1)}, bf16[2560,256]{1,0:T(8,128)(2,1)S(1)}, s32[]{:T(128)}) %tuple.61), condition=%wide.region_2.3_spmd, body=%wide.region_1.2_spmd.sunk | while | flops 1345060864 | bytes 1847873 | solution.py:65
  98.5 2.6 %fusion.64 = bf16[3,1024,256]{2,1,0:T(8,128)(2,1)} fusion(bf16[3,1024,256]{2,1,0:T(8,128)(2,1)} %get-tuple-element.174, s32[]{:T(128)} %get-tuple-element.173, bf16[2560,256]{1,0:T(8,128)(2,1)S(1)} %get-tuple-element.181, s32[1024]{0:T(1024)S(1)} %bitcast.130), kind=kOutput, calls=%fused_computation.5.clone.1 | convolution fusion | flops 1345060864 | bytes 1839616 | tf_op jit(solution)/shard_map/while/body/eval_jaxpr/dot_general | solution.py:63
  101.1 2.6 %fusion.64 = bf16[3,1024,256]{2,1,0:T(8,128)(2,1)} fusion(bf16[3,1024,256]{2,1,0:T(8,128)(2,1)} %get-tuple-element.174, s32[]{:T(128)} %get-tuple-element.173, bf16[2560,256]{1,0:T(8,128)(2,1)S(1)} %get-tuple-element.181, s32[1024]{0:T(1024)S(1)} %bitcast.130), kind=kOutput, calls=%fused_computation.5.clone.1 | convolution fusion | flops 1345060864 | bytes 1839616 | tf_op jit(solution)/shard_map/while/body/eval_jaxpr/dot_general | solution.py:63
  103.8 2.6 %fusion.64 = bf16[3,1024,256]{2,1,0:T(8,128)(2,1)} fusion(bf16[3,1024,256]{2,1,0:T(8,128)(2,1)} %get-tuple-element.174, s32[]{:T(128)} %get-tuple-element.173, bf16[2560,256]{1,0:T(8,128)(2,1)S(1)} %get-tuple-element.181, s32[1024]{0:T(1024)S(1)} %bitcast.130), kind=kOutput, calls=%fused_computation.5.clone.1 | convolution fusion | flops 1345060864 | bytes 1839616 | tf_op jit(solution)/shard_map/while/body/eval_jaxpr/dot_general | solution.py:63
  106.4 4.6 %reshape.131 = bf16[6,512,4,64]{3,2,1,0:T(4,128)(2,1)S(1)} reshape(bf16[3,1024,256]{2,1,0:T(8,128)(2,1)} %get-tuple-element.58) | data formatting | bytes 3145728 | tf_op jit(solution)/shard_map/reshape;reshape | solution.py:180
  111.0 1.9 %multiply_reduce_fusion.2 = bf16[512,4,64]{0,2,1:T(8,128)(2,1)} fusion(bf16[6,512,4,64]{3,2,1,0:T(4,128)(2,1)S(1)} %reshape.131, f32[6,512]{1,0:T(8,128)S(1)} %select_reduce_fusion, bf16[6,64,64]{2,1,0:T(8,128)(2,1)S(1)} %copy-done), kind=kOutput, calls=%fused_computation.23 | convolution fusion | flops 102105088 | bytes 1896448 | tf_op jit(solution)/shard_map/fcsj,fij->fcsi/dot_general | solution.py:178
  112.9 1.3 copy.96
  114.2 7.8 %fusion.46 = f32[512,4,64]{2,1,0:T(4,128)S(1)} fusion(bf16[512,4,64]{2,1,0:T(4,128)(2,1)S(1)} %copy.96, bf16[512,64,64]{2,1,0:T(8,128)(2,1)} %copy.91), kind=kOutput, calls=%fused_computation.99 | convolution fusion | flops 16777216 | bytes 4980736 | tf_op jit(solution)/shard_map/cij,csj->csi/dot_general | solution.py:185
  122.0 0.4 copy.98
  122.8 5.9 %collective-permute-start.8 = (bf16[1,2,32,256]{3,2,1,0:T(8,128)(2,1)S(1)}, bf16[1,2,32,256]{3,2,1,0:T(8,128)(2,1)S(1)}, u32[]{:S(2)}, u32[]{:S(2)}) collective-permute-start(bf16[1,2,32,256]{3,2,1,0:T(8,128)(2,1)S(1)} %maximum_bitcast_fusion), channel_id=1, source_target_pairs={{0,8},{8,16},{16,24},{1,9},{9,17},{17,25},{2,10},{10,18},{18,26},{... | collective-permute-start | bytes 98312 | tf_op jit(solution)/shard_map/ppermute | solution.py:19
  128.7 1.3 collective-permute-start.9
  130.4 1.0 copy.104
  131.4 0.4 collective-permute-done.9
  131.8 1.3 collective-permute-start.11
  133.1 5.0 %collective-permute-start.10 = (bf16[4,1,32,256]{3,2,1,0:T(8,128)(2,1)S(1)}, bf16[4,1,32,256]{3,2,1,0:T(8,128)(2,1)S(1)}, u32[]{:S(2)}, u32[]{:S(2)}) collective-permute-start(bf16[4,1,32,256]{3,2,1,0:T(8,128)(2,1)S(1)} %get-tuple-element.106), channel_id=1, source_target_pairs={{0,1},{1,2},{2,3},{3,4},{4,5},{5,6},{6,7},{8,9},{9,10},{10,11},{11... | collective-permute-start | bytes 196616 | tf_op jit(solution)/shard_map/ppermute | solution.py:19
  138.2 2.2 %collective-permute-done.10 = bf16[4,1,32,256]{3,2,1,0:T(8,128)(2,1)S(1)} collective-permute-done((bf16[4,1,32,256]{3,2,1,0:T(8,128)(2,1)S(1)}, bf16[4,1,32,256]{3,2,1,0:T(8,128)(2,1)S(1)}, u32[]{:S(2)}, u32[]{:S(2)}) %collective-permute-start.10) | collective-permute-done | bytes 65568 | tf_op jit(solution)/shard_map/ppermute | solution.py:19
  140.8 5.8 %while.25 = (s32[]{:T(128)}, bf16[4,1024,256]{2,1,0:T(8,128)(2,1)}, s32[4,1024]{1,0:T(4,128)S(1)}, bf16[640,256]{1,0:T(8,128)(2,1)S(1)}, s32[]{:T(128)}) while((s32[]{:T(128)}, bf16[4,1024,256]{2,1,0:T(8,128)(2,1)}, s32[4,1024]{1,0:T(4,128)S(1)}, bf16[640,256]{1,0:T(8,128)(2,1)S(1)}, s32[]{:T(128)}) %tuple.58), condition=%wide.region_6.7_spmd, body=%wide.region_5.6_spmd.sunk | while | flops 336461824 | bytes 864833 | solution.py:65
  140.8 1.4 fusion.66
  142.3 1.4 fusion.66
  143.8 1.4 fusion.66
  145.2 1.4 fusion.66
  146.7 3.4 %copy.101 = bf16[4,1024,256]{1,0,2:T(4,128)(2,1)S(1)} copy(bf16[4,1024,256]{2,1,0:T(8,128)(2,1)} %get-tuple-element.59) | data formatting | bytes 4194304 | tf_op jit(solution)/shard_map/while | solution.py:65
  150.0 2.8 %reshape.129 = bf16[4096,4,64,1]{0,2,1,3:T(8,128)(2,1)} reshape(bf16[4,1024,256]{1,0,2:T(4,128)(2,1)S(1)} %copy.101) | data formatting | bytes 4194304 | tf_op jit(solution)/shard_map/dot_general | solution.py:43
  152.8 6.8 %multiply_reduce_fusion = bf16[4096,4,64]{0,2,1:T(8,128)(2,1)S(1)} fusion(f32[4096,8]{0,1:T(8,128)S(1)} %copy-done.2, bf16[8,64,64,1]{2,1,0,3:T(8,128)(2,1)S(1)} %bitcast.128, bf16[4096,4,64,1]{0,2,1,3:T(8,128)(2,1)} %reshape.129), kind=kOutput, calls=%fused_computation.14 | convolution fusion | flops 1089470464 | bytes 4390912 | tf_op jit(solution)/shard_map/dot_general | solution.py:43
  159.6 2.5 %copy.105 = bf16[4096,256]{1,0:T(8,128)(2,1)} copy(bf16[4096,256]{0,1:T(8,128)(2,1)S(1)} %bitcast.122) | data formatting | bytes 4194304
  (72 shorter events, 2.1 us)
Async XLA Ops:
  0.6 110.4 %copy-start = (bf16[6,64,64]{2,1,0:T(8,128)(2,1)S(1)}, bf16[6,64,64]{2,1,0:T(8,128)(2,1)}, u32[]{:S(2)}) copy-start(bf16[6,64,64]{2,1,0:T(8,128)(2,1)} %param.22) | copy-start | bytes 147460
  1.4 3.1 %copy-start.1 = (f32[4096,8]{0,1:T(8,128)}, f32[4096,8]{0,1:T(8,128)S(1)}, u32[]{:S(2)}) copy-start(f32[4096,8]{0,1:T(8,128)S(1)} %fusion.30) | copy-start | bytes 393220
  1.4 3.1 %copy-start.5 = (s32[4096]{0:T(1024)S(1)}, s32[4096]{0:T(1024)}, u32[]{:S(2)}) copy-start(s32[4096]{0:T(1024)} %param.16) | copy-start | bytes 49156
  1.4 3.1 %copy-start.8 = (s32[4096]{0:T(1024)S(1)}, s32[4096]{0:T(1024)}, u32[]{:S(2)}) copy-start(s32[4096]{0:T(1024)} %param.17) | copy-start | bytes 49156
  1.5 3.1 %copy-start.3 = (bf16[8,64,64]{2,1,0:T(8,128)(2,1)S(1)}, bf16[8,64,64]{2,1,0:T(8,128)(2,1)}, u32[]{:S(2)}) copy-start(bf16[8,64,64]{2,1,0:T(8,128)(2,1)} %param.20) | copy-start | bytes 196612
  11.6 30.4 %collective-permute-start = (f32[1,32,256]{2,1,0:T(8,128)S(1)}, f32[1,32,256]{2,1,0:T(8,128)S(1)}, u32[]{:S(2)}, u32[]{:S(2)}) collective-permute-start(f32[1,32,256]{2,1,0:T(8,128)S(1)} %get-tuple-element.108), channel_id=1, source_target_pairs={{0,1},{1,2},{2,3},{3,4},{4,5},{5,6},{6,7},{8,9},{9,10},{10,11},{11... | collective-permute-start | bytes 98312 | tf_op jit(solution)/shard_map/ppermute | solution.py:19
  16.4 25.6 %collective-permute-start.1 = (f32[1,32,256]{2,1,0:T(8,128)S(1)}, f32[1,32,256]{2,1,0:T(8,128)S(1)}, u32[]{:S(2)}, u32[]{:S(2)}) collective-permute-start(f32[1,32,256]{2,1,0:T(8,128)S(1)} %get-tuple-element.111), channel_id=1, source_target_pairs={{1,0},{2,1},{3,2},{4,3},{5,4},{6,5},{7,6},{9,8},{10,9},{11,10},{12... | collective-permute-start | bytes 98312 | tf_op jit(solution)/shard_map/ppermute | solution.py:21
  17.7 24.3 %collective-permute-start.2 = (f32[1,32,256]{2,1,0:T(8,128)S(1)}, f32[1,32,256]{2,1,0:T(8,128)S(1)}, u32[]{:S(2)}, u32[]{:S(2)}) collective-permute-start(f32[1,32,256]{2,1,0:T(8,128)S(1)} %get-tuple-element.110), channel_id=1, source_target_pairs={{0,8},{8,16},{16,24},{1,9},{9,17},{17,25},{2,10},{10,18},{18,26},{... | collective-permute-start | bytes 98312 | tf_op jit(solution)/shard_map/ppermute | solution.py:19
  19.2 22.8 %collective-permute-start.3 = (f32[1,32,256]{2,1,0:T(8,128)S(1)}, f32[1,32,256]{2,1,0:T(8,128)S(1)}, u32[]{:S(2)}, u32[]{:S(2)}) collective-permute-start(f32[1,32,256]{2,1,0:T(8,128)S(1)} %get-tuple-element.109), channel_id=1, source_target_pairs={{8,0},{16,8},{24,16},{9,1},{17,9},{25,17},{10,2},{18,10},{26,18},{... | collective-permute-start | bytes 98312 | tf_op jit(solution)/shard_map/ppermute | solution.py:21
  20.5 1.9 %copy-start.9 = (s32[4,32]{1,0:T(4,128)S(1)}, s32[4,32]{1,0:T(4,128)}, u32[]{:S(2)}) copy-start(s32[4,32]{1,0:T(4,128)} %param.18) | copy-start | bytes 1540
  50.6 16.7 %copy-start.6 = (s32[6,512]{1,0:T(8,128)S(1)}, s32[6,512]{1,0:T(8,128)}, u32[]{:S(2)}) copy-start(s32[6,512]{1,0:T(8,128)} %param.25) | copy-start | bytes 36868
  50.6 16.8 %copy-start.7 = (s32[6,512]{1,0:T(8,128)S(1)}, s32[6,512]{1,0:T(8,128)}, u32[]{:S(2)}) copy-start(s32[6,512]{1,0:T(8,128)} %param.24) | copy-start | bytes 36868
  50.6 16.8 %copy-start.10 = (f32[16]{0:T(128)S(1)}, f32[16]{0:T(128)}, u32[]{:S(2)}) copy-start(f32[16]{0:T(128)} %param.23) | copy-start | bytes 196
  50.9 5.9 %collective-permute-start.4 = (bf16[1,1,512,256]{2,3,1,0:T(8,128)(2,1)S(1)}, bf16[1,1,512,256]{2,3,1,0:T(8,128)(2,1)S(1)}, u32[]{:S(2)}, u32[]{:S(2)}) collective-permute-start(bf16[1,1,512,256]{2,3,1,0:T(8,128)(2,1)S(1)} %bitcast.117), channel_id=1, source_target_pairs={{0,8},{8,16},{16,24},{1,9},{9,17},{17,25},{2,10},{10,18},{18,26},{... | collective-permute-start | bytes 786440 | tf_op jit(solution)/shard_map/ppermute | solution.py:19
  55.6 4.7 %collective-permute-start.5 = (bf16[1,1,512,256]{2,3,1,0:T(8,128)(2,1)S(1)}, bf16[1,1,512,256]{2,3,1,0:T(8,128)(2,1)S(1)}, u32[]{:S(2)}, u32[]{:S(2)}) collective-permute-start(bf16[1,1,512,256]{2,3,1,0:T(8,128)(2,1)S(1)} %bitcast.118), channel_id=1, source_target_pairs={{8,0},{16,8},{24,16},{9,1},{17,9},{25,17},{10,2},{18,10},{26,18},{... | collective-permute-start | bytes 786440 | tf_op jit(solution)/shard_map/ppermute | solution.py:21
  60.3 35.5 %collective-permute-start.6 = (bf16[3,1,512,256]{2,3,1,0:T(8,128)(2,1)S(1)}, bf16[3,1,512,256]{2,3,1,0:T(8,128)(2,1)}, u32[]{:S(2)}, u32[]{:S(2)}) collective-permute-start(bf16[3,1,512,256]{2,3,1,0:T(8,128)(2,1)S(1)} %pad_maximum_fusion), channel_id=1, source_target_pairs={{0,1},{1,2},{2,3},{3,4},{4,5},{5,6},{6,7},{8,9},{9,10},{10,11},{11... | collective-permute-start | bytes 2359304 | tf_op jit(solution)/shard_map/ppermute | solution.py:19
  65.9 31.0 %collective-permute-start.7 = (bf16[3,1,512,256]{2,3,1,0:T(8,128)(2,1)S(1)}, bf16[3,1,512,256]{2,3,1,0:T(8,128)(2,1)}, u32[]{:S(2)}, u32[]{:S(2)}) collective-permute-start(bf16[3,1,512,256]{2,3,1,0:T(8,128)(2,1)S(1)} %pad_maximum_fusion), channel_id=1, source_target_pairs={{1,0},{2,1},{3,2},{4,3},{5,4},{6,5},{7,6},{9,8},{10,9},{11,10},{12... | collective-permute-start | bytes 2359304 | tf_op jit(solution)/shard_map/ppermute | solution.py:21
  122.0 8.0 %copy-start.4 = (bf16[8,64,64]{2,1,0:T(8,128)(2,1)S(1)}, bf16[8,64,64]{2,1,0:T(8,128)(2,1)}, u32[]{:S(2)}) copy-start(bf16[8,64,64]{2,1,0:T(8,128)(2,1)} %param.20) | copy-start | bytes 196612
  122.8 8.6 %collective-permute-start.8 = (bf16[1,2,32,256]{3,2,1,0:T(8,128)(2,1)S(1)}, bf16[1,2,32,256]{3,2,1,0:T(8,128)(2,1)S(1)}, u32[]{:S(2)}, u32[]{:S(2)}) collective-permute-start(bf16[1,2,32,256]{3,2,1,0:T(8,128)(2,1)S(1)} %maximum_bitcast_fusion), channel_id=1, source_target_pairs={{0,8},{8,16},{16,24},{1,9},{9,17},{17,25},{2,10},{10,18},{18,26},{... | collective-permute-start | bytes 98312 | tf_op jit(solution)/shard_map/ppermute | solution.py:19
  128.7 3.1 %collective-permute-start.9 = (bf16[1,2,32,256]{3,2,1,0:T(8,128)(2,1)S(1)}, bf16[1,2,32,256]{3,2,1,0:T(8,128)(2,1)S(1)}, u32[]{:S(2)}, u32[]{:S(2)}) collective-permute-start(bf16[1,2,32,256]{3,2,1,0:T(8,128)(2,1)S(1)} %maximum_bitcast_fusion.1), channel_id=1, source_target_pairs={{8,0},{16,8},{24,16},{9,1},{17,9},{25,17},{10,2},{18,10},{26,18},{... | collective-permute-start | bytes 98312 | tf_op jit(solution)/shard_map/ppermute | solution.py:21
  131.8 6.4 %collective-permute-start.11 = (bf16[4,1,32,256]{3,2,1,0:T(8,128)(2,1)S(1)}, bf16[4,1,32,256]{3,2,1,0:T(8,128)(2,1)S(1)}, u32[]{:S(2)}, u32[]{:S(2)}) collective-permute-start(bf16[4,1,32,256]{3,2,1,0:T(8,128)(2,1)S(1)} %get-tuple-element.107), channel_id=1, source_target_pairs={{1,0},{2,1},{3,2},{4,3},{5,4},{6,5},{7,6},{9,8},{10,9},{11,10},{12... | collective-permute-start | bytes 196616 | tf_op jit(solution)/shard_map/ppermute | solution.py:21
  133.1 7.4 %collective-permute-start.10 = (bf16[4,1,32,256]{3,2,1,0:T(8,128)(2,1)S(1)}, bf16[4,1,32,256]{3,2,1,0:T(8,128)(2,1)S(1)}, u32[]{:S(2)}, u32[]{:S(2)}) collective-permute-start(bf16[4,1,32,256]{3,2,1,0:T(8,128)(2,1)S(1)} %get-tuple-element.106), channel_id=1, source_target_pairs={{0,1},{1,2},{2,3},{3,4},{4,5},{5,6},{6,7},{8,9},{9,10},{10,11},{11... | collective-permute-start | bytes 196616 | tf_op jit(solution)/shard_map/ppermute | solution.py:19
  150.0 2.8 %copy-start.2 = (f32[4096,8]{0,1:T(8,128)S(1)}, f32[4096,8]{0,1:T(8,128)}, u32[]{:S(2)}) copy-start(f32[4096,8]{0,1:T(8,128)} %copy-done.1) | copy-start | bytes 393220
where the time goes:
time: 165 us; the launch traced here: 162 us
  matrix products  47.6 us (29%)
  local copies, waits for them, and re-layouts  42.4 us (26%)
  starting transfers between devices  35.3 us (21%)
  waiting for transfers between devices  34.3 us (21%)
    ppermute x6, waiting for transfers between devices, padded(): lax.ppermute(tail, axis, [(i, (i + 1) % count) for i in range(ends)])  30.5 us
    ppermute x6, starting transfers between devices, padded(): lax.ppermute(tail, axis, [(i, (i + 1) % count) for i in range(ends)])  27.4 us
    unnamed x30, local copies, waits for them, and re-layouts  15 us
    dot_general x8, matrix products, one_block(): jnp.dot(onehot, table, preferred_element_type=jnp.float32)  13.9 us
    reshape x1, local copies, waits for them, and re-layouts, shards(): inverse = inverse_blocks.reshape(coarse_count, order_dim, order_dim)  13 us
    dot_general x2, matrix products, typed_product(): jnp.dot(columns, stacked_table(matrices, flipped), preferred_element_type...  12.3 us
    ppermute x6, starting transfers between devices, padded(): lax.ppermute(head, axis, [((i + 1) % count, i) for i in range(ends)])  7.92 us
    dot_general x1, matrix products, shards(): jnp.einsum('cij,csj->csi', inverse, coarse_rhs.reshape(coarse_count, rhs_...  7.79 us
  transfers between devices with their start and end apart: 12, of which 5 were waited for; matrix products, arithmetic and copies ran while one was open for 15% of the time, Pallas kernels for 0%

commit v1 on v0

v1 whole, which is shorter than its diff:
```python
import functools

import jax
import jax.numpy as jnp
from jax import lax
from jax.experimental import pallas as pl
from jax.experimental.pallas import tpu as pltpu
from jax.sharding import PartitionSpec as P

omega = 0.5
MESH = pl.DeviceIdType.MESH
f32 = jnp.float32
bf16 = jnp.bfloat16
i32 = jnp.int32


def iota(shape, dim):
    return lax.broadcasted_iota(i32, shape, dim)


def nn(a, b):
    return lax.dot_general(a, b, (((1,), (0,)), ((), ())), preferred_element_type=f32)


def nt(a, b):
    return lax.dot_general(a, b, (((1,), (1,)), ((), ())), preferred_element_type=f32)


def onehot(mask):
    return jnp.where(mask, f32(1.0), f32(0.0)).astype(bf16)


def tiler(width, order):
    return onehot(lax.rem(iota((width, order), 0), order) == iota((width, order), 1))


def block_diagonal(matrix, width, flipped):
    order = matrix.shape[0]
    spread = tiler(width, order)
    if flipped:
        half = nt(spread, matrix)
    else:
        half = nn(spread, matrix)
    full = nt(half.astype(bf16), spread)
    same = lax.div(iota((width, width), 0), order) == lax.div(iota((width, width), 1), order)
    return jnp.where(same, full, f32(0.0)).astype(bf16)


def columns_of(row):
    parts = [
        jnp.transpose(jnp.broadcast_to(row[:, at : at + 128], (128, 128)))
        for at in range(0, row.shape[1], 128)
    ]
    return jnp.concatenate(parts, axis=0)


def target_rows(owner, slot, me, coarse, ghost):
    offset = owner - me
    direction = jnp.where(offset == -1, 0, jnp.where(offset == 1, 1, jnp.where(offset < 0, 2, 3)))
    return jnp.where(offset == 0, slot, coarse + direction * ghost + slot)


def typed_sum(rows, kinds, tables, width, count):
    wide = jnp.concatenate([kinds] * (width // 128), axis=1)
    rows = rows.astype(f32)
    total = None
    for kind in range(count):
        part = nn(
            jnp.where(wide == kind, rows, f32(0.0)).astype(bf16),
            tables[kind * width : (kind + 1) * width, :],
        )
        total = part if total is None else total + part
    return total


def restrict_kernel(
    geometry, fine_ref, owner_ref, slot_ref, kind_ref, table_ref, inverse_ref,
    local_ref, out_ref, turned_ref, tables, perm, total,
):
    coarse, ghost, width, order, kinds, n_py = geometry
    me = lax.axis_index("px") * n_py + lax.axis_index("py")
    step = pl.program_id(0)
    half = 8 * order

    @pl.when(step == 0)
    def _():
        for kind in range(kinds):
            tables[kind * width : (kind + 1) * width, :] = block_diagonal(
                table_ref[kind], width, True
            )
        at = iota((half, half), 0)
        perm[...] = onehot(
            iota((half, half), 1) == lax.rem(at, 8) * order + lax.div(at, 8)
        )
        total[...] = jnp.zeros_like(total)

    chunk = fine_ref.shape[0]
    for begin in range(0, chunk, 512):
        span = slice(begin, begin + 512)
        contrib = typed_sum(
            fine_ref[span, :], columns_of(kind_ref[:, span]), tables, width, kinds
        ).astype(bf16)
        target = target_rows(owner_ref[:, span], slot_ref[:, span], me, coarse, ghost)
        rows = coarse + 4 * ghost
        total[...] += nn(onehot(iota((rows, 512), 0) == target), contrib)

    halves = [
        nt(perm[...], inverse_ref[:, at * half : (at + 1) * half]).reshape(order, 8, coarse)
        for at in range(2)
    ]
    turned_ref[...] = jnp.concatenate(halves, axis=1).astype(bf16)

    @pl.when(step == pl.num_programs(0) - 1)
    def _():
        local_ref[...] = total[:coarse, :]
        out_ref[...] = total[coarse:, :].astype(bf16)


def coarse_kernel(
    geometry, local_ref, outgoing, ghost_row_ref, turned, face_ref, coef_ref, index_ref,
    neighbour_ref, solution_ref, returned,
    incoming, reply, xt, first_t, near, code, beside,
    ghost_send, ghost_recv, reply_send, reply_recv, halo_send, halo_recv,
):
    coarse, ghost, width, order, n_px, n_py, kinds = geometry
    rhs = width // order
    faces = face_ref.shape[0]
    px = lax.axis_index("px")
    py = lax.axis_index("py")
    me = px * n_py + py
    exists = [py > 0, py < n_py - 1, px > 0, px < n_px - 1]
    place = [(px, py - 1), (px, py + 1), (px - 1, py), (px + 1, py)]
    far = [(py > 1, (px, py - 2)), (py < n_py - 2, (px, py + 2))]

    for slot, there in enumerate(exists):
        @pl.when(jnp.logical_not(there))
        def _():
            near[slot + 1] = jnp.zeros((coarse, width), bf16)
            incoming[pl.ds(slot * ghost, ghost), :] = jnp.zeros((ghost, width), bf16)
            returned[pl.ds(slot * ghost, ghost), :] = jnp.zeros((ghost, width), bf16)

    barrier = pltpu.get_barrier_semaphore()
    everyone = list(zip(exists, place)) + far
    for there, where in everyone:
        @pl.when(there)
        def _():
            pl.semaphore_signal(barrier, inc=1, device_id=where, device_id_type=MESH)
    pl.semaphore_wait(barrier, sum(there.astype(i32) for there, _ in everyone))

    def lists(source, target, send, recv, at, to):
        return pltpu.make_async_remote_copy(
            src_ref=source.at[pl.ds(at * ghost, ghost)],
            dst_ref=target.at[pl.ds(to * ghost, ghost)],
            send_sem=send.at[at],
            recv_sem=recv.at[to],
            device_id=place[at],
            device_id_type=MESH,
        )

    def start_lists(source, target, send, recv):
        for at in range(4):
            @pl.when(exists[at])
            def _():
                lists(source, target, send, recv, at, at ^ 1).start()

    def finish_lists(source, target, send, recv):
        for at in range(4):
            @pl.when(exists[at])
            def _():
                lists(source, target, send, recv, at, at).wait_recv()
                lists(source, target, send, recv, at, at ^ 1).wait_send()

    start_lists(outgoing, incoming, ghost_send, ghost_recv)

    offset = lax.shift_right_logical(neighbour_ref[...], coarse.bit_length() - 1) - me
    slot = jnp.where(
        offset == 0, 0,
        jnp.where(offset == -1, 1, jnp.where(offset == 1, 2, jnp.where(offset < 0, 3, 4))),
    )
    codes = slot * coarse + (neighbour_ref[...] & (coarse - 1))
    for face in range(faces):
        code[face * coarse : (face + 1) * coarse, :] = columns_of(codes[face : face + 1, :])
    scales = jnp.zeros(index_ref.shape, f32)
    for kind in range(kinds):
        scales = jnp.where(index_ref[...] == kind, coef_ref[0, kind], scales)
    lists_onehot = onehot(iota((coarse, 4 * ghost), 0) == ghost_row_ref[...])
    pick_onehot = onehot(
        jnp.concatenate([columns_of(ghost_row_ref[...])] * (coarse // 128), axis=1)
        == iota((4 * ghost, coarse), 1)
    )

    finish_lists(outgoing, incoming, ghost_send, ghost_recv)
    rhs_rows = local_ref[...] + nn(lists_onehot, incoming[...])
    xt[...] = jnp.transpose(rhs_rows.astype(bf16).astype(f32))

    def sweep(tile):
        lanes = slice(tile * 128, (tile + 1) * 128)

        def body(block, sums):
            sums = list(sums)
            values = [
                xt[pl.ds(pl.multiple_of(s * order + block * 8, 8), 8), lanes] for s in range(rhs)
            ]
            for inner in range(8):
                at = block * 8 + inner
                matrix = turned[at, :, lanes].astype(f32)
                for s in range(rhs):
                    sums[s] = sums[s] + matrix * values[s][inner : inner + 1, :]
            return tuple(sums)

        start = tuple(jnp.zeros((order, 128), f32) for _ in range(rhs))
        return jnp.concatenate(lax.fori_loop(0, order // 8, body, start), axis=0)

    even = lax.rem(py, 2) == 0
    partner = jnp.where(even, 2, 1)
    beyond = 3 - partner
    partner_place = (px, jnp.where(even, py + 1, py - 1))
    relay_place = (px, jnp.where(even, py + 2, py - 2))
    relays = jnp.where(even, py + 2, n_py + 1 - py) < n_py
    gets_relay = jnp.where(even, py - 2, n_py - 3 - py) >= 0

    def halo(role, tile, source, target, where):
        rows = pl.ds(tile * 128, 128)
        return pltpu.make_async_remote_copy(
            src_ref=near.at[source, rows],
            dst_ref=near.at[target, rows],
            send_sem=halo_send.at[role, tile],
            recv_sem=halo_recv.at[role, tile],
            device_id=where,
            device_id_type=MESH,
        )

    def to_partner(tile):
        return halo(0, tile, 0, beyond, partner_place)

    def from_partner(tile):
        return halo(0, tile, 0, partner, partner_place)

    def onward(tile):
        return halo(1, tile, partner, beyond, relay_place)

    def from_relay(tile):
        return halo(1, tile, partner, beyond, relay_place)

    def lower(tile):
        return halo(2, tile, 0, 4, place[2])

    def upper(tile):
        return halo(3, tile, 0, 3, place[3])

    tiles = coarse // 128
    for tile in range(tiles):
        lanes = slice(tile * 128, (tile + 1) * 128)
        rounded = sweep(tile).astype(bf16).astype(f32)
        first_t[:, lanes] = rounded
        near[0, lanes, :] = jnp.transpose(rounded).astype(bf16)
        to_partner(tile).start()

        @pl.when(exists[2])
        def _():
            lower(tile).start()

        @pl.when(exists[3])
        def _():
            upper(tile).start()

    step_rows = 256
    steps = faces * coarse // step_rows

    def gather(block, begin, end, fresh):
        def body(step, _):
            rows = pl.ds(pl.multiple_of(step * step_rows, step_rows), step_rows)
            here = code[rows, :] - block * coarse
            lane = iota((step_rows, 128), 1)
            picks = jnp.concatenate(
                [onehot(here == lane + at * 128) for at in range(tiles)], axis=1
            )
            found = nn(picks, near[block])
            if fresh:
                beside[rows, :] = found
            else:
                beside[rows, :] += found
            return 0

        lax.fori_loop(begin, end, body, 0)

    for tile in range(tiles):
        from_partner(tile).wait_recv()

        @pl.when(relays)
        def _():
            onward(tile).start()
        gather(0, tile * steps // tiles, (tile + 1) * steps // tiles, True)
    gather(partner, 0, steps, False)

    @pl.when(exists[2])
    def _():
        for tile in range(tiles):
            halo(3, tile, 0, 3, place[2]).wait_recv()
    gather(3, 0, steps, False)

    @pl.when(exists[3])
    def _():
        for tile in range(tiles):
            halo(2, tile, 0, 4, place[3]).wait_recv()
    gather(4, 0, steps, False)

    @pl.when(gets_relay)
    def _():
        for tile in range(tiles):
            from_relay(tile).wait_recv()
    gather(beyond, 0, steps, False)

    coupled = jnp.zeros((width, coarse), f32)
    for face in range(faces):
        matrix = block_diagonal(face_ref[face], width, False)
        rows = slice(face * coarse, (face + 1) * coarse)
        coupled += nt(matrix, beside[rows, :].astype(bf16)) * scales[face : face + 1, :]
    xt[...] = coupled.astype(bf16).astype(f32)

    for tile in range(tiles):
        lanes = slice(tile * 128, (tile + 1) * 128)
        solved = first_t[:, lanes] - omega * sweep(tile)
        solution_ref[lanes, :] = jnp.transpose(solved)

    reply[...] = nn(pick_onehot, solution_ref[...].astype(bf16)).astype(bf16)
    start_lists(reply, returned, reply_send, reply_recv)
    for tile in range(tiles):
        to_partner(tile).wait_send()

        @pl.when(relays)
        def _():
            onward(tile).wait_send()

        @pl.when(exists[2])
        def _():
            lower(tile).wait_send()

        @pl.when(exists[3])
        def _():
            upper(tile).wait_send()
    finish_lists(reply, returned, reply_send, reply_recv)


def prolong_kernel(
    geometry, solution_ref, returned_ref, owner_ref, slot_ref, kind_ref, table_ref,
    out_solution_ref, fine_ref, tables, held,
):
    coarse, ghost, width, order, kinds, n_py = geometry
    me = lax.axis_index("px") * n_py + lax.axis_index("py")
    step = pl.program_id(0)

    @pl.when(step == 0)
    def _():
        for kind in range(kinds):
            tables[kind * width : (kind + 1) * width, :] = block_diagonal(
                table_ref[kind], width, False
            )
        held[:coarse, :] = solution_ref[...].astype(bf16)
        held[coarse:, :] = returned_ref[...]
        out_solution_ref[...] = solution_ref[...]

    rows = coarse + 4 * ghost
    target = columns_of(target_rows(owner_ref[...], slot_ref[...], me, coarse, ghost))
    lane = iota(target.shape, 1)
    picks = jnp.concatenate([onehot(target == lane + at) for at in range(0, rows, 128)], axis=1)
    fetched = nn(picks, held[...]).astype(bf16)
    fine_ref[...] = typed_sum(
        fetched, columns_of(kind_ref[...]), tables, width, kinds
    ).astype(bf16)


def shards(
    n_px, n_py,
    fine_residual, dest_owner, coarse_slot, ghost_slot, child_type, restrict_table,
    inverse_blocks, face_table, face_coef, coef_index, neighbours,
):
    fine, width = fine_residual.shape
    coarse = inverse_blocks.shape[0]
    ghost = ghost_slot.shape[1]
    kinds, order, _ = restrict_table.shape
    faces = face_table.shape[0]
    owner = dest_owner.reshape(1, fine)
    slot = coarse_slot.reshape(1, fine)
    kind = child_type.reshape(1, fine)
    whole = pl.BlockSpec(memory_space=pltpu.VMEM)
    grant = 48 * 1024 * 1024

    steps = order // 16
    chunk = fine // steps
    geometry = (coarse, ghost, width, order, kinds, n_py)
    row = pl.BlockSpec((1, chunk), lambda i: (0, i))
    local, outgoing, turned = pl.pallas_call(
        functools.partial(restrict_kernel, geometry),
        grid=(steps,),
        in_specs=[
            pl.BlockSpec((chunk, width), lambda i: (i, 0)),
            row, row, row,
            pl.BlockSpec((kinds, order, order), lambda i: (0, 0, 0)),
            pl.BlockSpec((coarse, 16 * order), lambda i: (0, i)),
        ],
        out_specs=[
            pl.BlockSpec((coarse, width), lambda i: (0, 0)),
            pl.BlockSpec((4 * ghost, width), lambda i: (0, 0)),
            pl.BlockSpec((order, 16, coarse), lambda i: (0, i, 0)),
        ],
        out_shape=[
            jax.ShapeDtypeStruct((coarse, width), f32),
            jax.ShapeDtypeStruct((4 * ghost, width), bf16),
            jax.ShapeDtypeStruct((order, order, coarse), bf16),
        ],
        scratch_shapes=[
            pltpu.VMEM((kinds * width, width), bf16),
            pltpu.VMEM((8 * order, 8 * order), bf16),
            pltpu.VMEM((coarse + 4 * ghost, width), f32),
        ],
        compiler_params=pltpu.CompilerParams(vmem_limit_bytes=grant),
        name="restrict",
    )(fine_residual, owner, slot, kind, restrict_table, inverse_blocks)

    tiles = coarse // 128
    solved, returned = pl.pallas_call(
        functools.partial(
            coarse_kernel, (coarse, ghost, width, order, n_px, n_py, face_coef.shape[0])
        ),
        in_specs=[whole] * 5 + [pl.BlockSpec(memory_space=pltpu.SMEM)] + [whole] * 2,
        out_specs=[whole] * 2,
        out_shape=[
            jax.ShapeDtypeStruct((coarse, width), f32),
            jax.ShapeDtypeStruct((4 * ghost, width), bf16),
        ],
        scratch_shapes=[
            pltpu.VMEM((4 * ghost, width), bf16),
            pltpu.VMEM((4 * ghost, width), bf16),
            pltpu.VMEM((width, coarse), f32),
            pltpu.VMEM((width, coarse), f32),
            pltpu.VMEM((5, coarse, width), bf16),
            pltpu.VMEM((faces * coarse, 128), i32),
            pltpu.VMEM((faces * coarse, width), f32),
        ]
        + [pltpu.SemaphoreType.DMA((4,))] * 4
        + [pltpu.SemaphoreType.DMA((4, tiles))] * 2,
        compiler_params=pltpu.CompilerParams(
            collective_id=0, has_side_effects=True, vmem_limit_bytes=grant
        ),
        name="coarse",
    )(
        local, outgoing, ghost_slot.reshape(1, 4 * ghost), turned, face_table,
        face_coef.reshape(1, -1), coef_index, neighbours,
    )

    chunk = 512
    row = pl.BlockSpec((1, chunk), lambda i: (0, i))
    return pl.pallas_call(
        functools.partial(prolong_kernel, geometry),
        grid=(fine // chunk,),
        in_specs=[
            pl.BlockSpec((coarse, width), lambda i: (0, 0)),
            pl.BlockSpec((4 * ghost, width), lambda i: (0, 0)),
            row, row, row,
            pl.BlockSpec((kinds, order, order), lambda i: (0, 0, 0)),
        ],
        out_specs=[
            pl.BlockSpec((coarse, width), lambda i: (0, 0)),
            pl.BlockSpec((chunk, width), lambda i: (i, 0)),
        ],
        out_shape=[
            jax.ShapeDtypeStruct((coarse, width), f32),
            jax.ShapeDtypeStruct((fine, width), bf16),
        ],
        scratch_shapes=[
            pltpu.VMEM((kinds * width, width), bf16),
            pltpu.VMEM((coarse + 4 * ghost, width), bf16),
        ],
        compiler_params=pltpu.CompilerParams(vmem_limit_bytes=grant),
        name="prolong",
    )(solved, returned, owner, slot, kind, restrict_table)


def solution(mesh):
    both = ("px", "py")
    in_specs = (
        P(both, None), P(both), P(both), P(both, None), P(both), P(), P(both, None), P(), P(),
        P(None, both), P(None, both),
    )
    out_specs = (P(both, None), P(both, None))
    return jax.shard_map(
        functools.partial(shards, mesh.shape["px"], mesh.shape["py"]),
        mesh=mesh, in_specs=in_specs, out_specs=out_specs, check_vma=False,
    )
```

time: 165 us -> 75.4 us (0.46); the launches traced: 162 us -> 74.9 us
  Pallas kernels: 0 us -> 66.6 us
  matrix products: 47.6 us -> 0 us
  starting transfers between devices: 35.3 us -> 0 us
  local copies, waits for them, and re-layouts: 42.4 us -> 7.63 us
  waiting for transfers between devices: 34.3 us -> 0 us
    pallas_call x0 -> x3, Pallas kernels: none -> 66.6 us  [the longest x1 36.6 us: shards(): pl.pallas_call(functools.partial(coarse_kernel, (coarse, ghost, width, or...]
    dot_general x16 -> x0, matrix products: 47.6 us -> none  [the longest x8 13.9 us: one_block(): jnp.dot(onehot, table, preferred_element_type=jnp.float32)]
    ppermute x12 -> x0, starting transfers between devices: 35.3 us -> none  [the longest x6 27.4 us: padded(): lax.ppermute(tail, axis, [(i, (i + 1) % count) for i in range(ends)])]
    ppermute x12 -> x0, waiting for transfers between devices: 34.3 us -> none  [the longest x6 30.5 us: padded(): lax.ppermute(tail, axis, [(i, (i + 1) % count) for i in range(ends)])]
    reshape x5 -> x1, local copies, waits for them, and re-layouts: 13.6 us -> 0.77 us  [shards(): ghost_slot.reshape(1, 4 * ghost)]
    unnamed x30 -> x28, local copies, waits for them, and re-layouts: 15 us -> 6.86 us
    another operation x8 -> x0, local copies, waits for them, and re-layouts: 5.24 us -> none  [the longest x1 4.59 us: shards(): beside.reshape(faces_count, coarse_count, rhs_count, order_dim)]
    dot_general x4 -> x0, local copies, waits for them, and re-layouts: 3.57 us -> none  [the longest x2 2.89 us: typed_product(): jnp.dot(columns, stacked_table(matrices, flipped), preferred_element_type...]
  transfers between devices with their start and end apart: 12 -> 0, of which waited for: 5 -> 0; matrix products, arithmetic and copies ran while one was open for 15% -> 0% of each run, Pallas kernels for 0% -> 0%
where the time goes in v1:
time: 75.4 us; the launch traced here: 74.9 us
  Pallas kernels  66.6 us (88%)
  local copies, waits for them, and re-layouts  7.63 us (10%)
    pallas_call x1, Pallas kernels, shards(): pl.pallas_call(functools.partial(coarse_kernel, (coarse, ghost, width, or...  36.6 us
    pallas_call x1, Pallas kernels, shards(): pl.pallas_call(functools.partial(restrict_kernel, geometry), grid=(steps,...  16.9 us
    pallas_call x1, Pallas kernels, shards(): pl.pallas_call(functools.partial(prolong_kernel, geometry), grid=(fine //...  13.1 us
    unnamed x28, local copies, waits for them, and re-layouts  6.86 us

profile of v1, /device:TPU:0, one launch (start us, length us, event | category | flops | bytes accessed | tf_op | source)
XLA Modules:
  0.0 74.9 jit_solution(17575216416455539138)
XLA Ops:
  0.6 0.0 copy-start.13
  0.6 0.8 %reshape.22.ghost_row_ref = s32[1,128]{1,0:T(1,128)S(1)} reshape(s32[4,32]{1,0:T(4,128)} %param.14) | data formatting | bytes 1024 | tf_op jit(solution)/shard_map/reshape | solution.py:448
  1.4 0.0 copy-start.1
  1.4 1.6 %copy-done.1 = bf16[4096,256]{1,0:T(8,128)(2,1)S(1)} copy-done((bf16[4096,256]{1,0:T(8,128)(2,1)S(1)}, bf16[4096,256]{1,0:T(8,128)(2,1)}, u32[]{:S(2)}) %copy-start.1) | copy-done | bytes 2097176
  3.0 0.0 copy-start.2
  3.0 0.9 %copy-done.2 = bf16[8,64,64]{2,1,0:T(8,128)(2,1)S(1)} copy-done((bf16[8,64,64]{2,1,0:T(8,128)(2,1)S(1)}, bf16[8,64,64]{2,1,0:T(8,128)(2,1)}, u32[]{:S(2)}) %copy-start.2) | copy-done | bytes 65560
  3.9 0.0 copy-start.5
  3.9 0.7 copy-done.5
  4.6 0.0 copy-start.7
  4.6 0.7 copy-done.7
  5.3 0.0 copy-start.9
  5.3 0.7 copy-done.9
  6.1 0.0 copy-start.4
  6.1 0.0 copy-start.11
  6.1 0.0 copy-start.12
  6.1 0.0 copy-start.3
  6.1 0.0 copy-start.6
  6.1 0.0 copy-start.8
  6.1 0.0 copy-start.10
  6.1 16.9 %restrict.1 = (f32[512,256]{1,0:T(8,128)S(1)}, bf16[128,256]{1,0:T(8,128)(2,1)S(1)}, bf16[64,64,512]{2,1,0:T(8,128)(2,1)}) custom-call(bf16[4096,256]{1,0:T(8,128)(2,1)S(1)} %copy-done.1, s32[1,4096]{1,0:T(1,128)S(1)} %bitcast.4, s32[1,4096]{1,0:T(1,128)S(1)} %bitcast.6, s32[1,4096]{1,0:T(1,128)S(1)} %bitcast.8, bf16[8,64,64]{2,1,0:T(8,128)(2,1)S(1)} %copy-done.2, ...), custom_call_target="tpu_custom_call" | custom-call | tf_op jit(solution)/shard_map/restrict/pallas_call | solution.py:393
  23.0 0.0 copy-done.13
  23.0 0.0 copy-done.4
  23.0 0.0 copy-done.11
  23.0 0.0 copy-done.12
  23.0 0.0 copy-start
  23.0 2.2 %copy-done = bf16[64,64,512]{2,1,0:T(8,128)(2,1)S(1)} copy-done((bf16[64,64,512]{2,1,0:T(8,128)(2,1)S(1)}, bf16[64,64,512]{2,1,0:T(8,128)(2,1)}, u32[]{:S(2)}) %copy-start) | copy-done | bytes 4194328
  25.2 36.6 %coarse.1 = (f32[512,256]{1,0:T(8,128)S(1)}, bf16[128,256]{1,0:T(8,128)(2,1)S(1)}) custom-call(f32[512,256]{1,0:T(8,128)S(1)} %get-tuple-element.7.local_ref, bf16[128,256]{1,0:T(8,128)(2,1)S(1)} %get-tuple-element.8.outgoing, s32[1,128]{1,0:T(1,128)S(1)} %reshape.22.ghost_row_ref, bf16[64,64,512]{2,1,0:T(8,128)(2,1)S(1)} %copy-done, ...), custom_call_target="tpu_custom_call" | custom-call | tf_op jit(solution)/shard_map/coarse/pallas_call | solution.py:422
  61.8 0.0 copy-done.3
  61.8 0.0 copy-done.6
  61.8 0.0 copy-done.8
  61.8 0.0 copy-done.10
  61.9 13.1 %prolong.1 = (f32[512,256]{1,0:T(8,128)}, bf16[4096,256]{1,0:T(8,128)(2,1)}) custom-call(f32[512,256]{1,0:T(8,128)S(1)} %get-tuple-element.10.solution_ref, bf16[128,256]{1,0:T(8,128)(2,1)S(1)} %get-tuple-element.11.returned_ref, s32[1,4096]{1,0:T(1,128)S(1)} %bitcast.5, s32[1,4096]{1,0:T(1,128)S(1)} %bitcast.7, s32[1,4096]{1,0:T(1,128)S(1)} %bitcast.9, ...), custom_call_target="tpu_custom_call" | custom-call | tf_op jit(solution)/shard_map/prolong/pallas_call | solution.py:454
Async XLA Ops:
  0.6 22.3 %copy-start.13 = (f32[16]{0:T(128)S(1)}, f32[16]{0:T(128)}, u32[]{:S(2)}) copy-start(f32[16]{0:T(128)} %param.19) | copy-start | bytes 196
  1.4 1.6 %copy-start.1 = (bf16[4096,256]{1,0:T(8,128)(2,1)S(1)}, bf16[4096,256]{1,0:T(8,128)(2,1)}, u32[]{:S(2)}) copy-start(bf16[4096,256]{1,0:T(8,128)(2,1)} %fine_ref.1) | copy-start | bytes 6291460
  3.0 0.9 %copy-start.2 = (bf16[8,64,64]{2,1,0:T(8,128)(2,1)S(1)}, bf16[8,64,64]{2,1,0:T(8,128)(2,1)}, u32[]{:S(2)}) copy-start(bf16[8,64,64]{2,1,0:T(8,128)(2,1)} %table_ref.3) | copy-start | bytes 196612
  3.9 0.7 copy-start.5
  4.6 0.7 copy-start.7
  5.3 0.7 copy-start.9
  6.1 16.9 %copy-start.4 = (bf16[6,64,64]{2,1,0:T(8,128)(2,1)S(1)}, bf16[6,64,64]{2,1,0:T(8,128)(2,1)}, u32[]{:S(2)}) copy-start(bf16[6,64,64]{2,1,0:T(8,128)(2,1)} %face_ref.1) | copy-start | bytes 147460
  6.1 16.9 %copy-start.11 = (s32[6,512]{1,0:T(8,128)S(1)}, s32[6,512]{1,0:T(8,128)}, u32[]{:S(2)}) copy-start(s32[6,512]{1,0:T(8,128)} %index_ref.1) | copy-start | bytes 36868
  6.1 16.9 %copy-start.12 = (s32[6,512]{1,0:T(8,128)S(1)}, s32[6,512]{1,0:T(8,128)}, u32[]{:S(2)}) copy-start(s32[6,512]{1,0:T(8,128)} %neighbour_ref.1) | copy-start | bytes 36868
  6.1 55.8 %copy-start.3 = (bf16[8,64,64]{2,1,0:T(8,128)(2,1)S(1)}, bf16[8,64,64]{2,1,0:T(8,128)(2,1)}, u32[]{:S(2)}) copy-start(bf16[8,64,64]{2,1,0:T(8,128)(2,1)} %table_ref.3) | copy-start | bytes 196612
  6.1 55.8 %copy-start.6 = (s32[4096]{0:T(1024)S(1)}, s32[4096]{0:T(1024)}, u32[]{:S(2)}) copy-start(s32[4096]{0:T(1024)} %param.12) | copy-start | bytes 49156
  6.1 55.8 %copy-start.8 = (s32[4096]{0:T(1024)S(1)}, s32[4096]{0:T(1024)}, u32[]{:S(2)}) copy-start(s32[4096]{0:T(1024)} %param.13) | copy-start | bytes 49156
  6.1 55.8 %copy-start.10 = (s32[4096]{0:T(1024)S(1)}, s32[4096]{0:T(1024)}, u32[]{:S(2)}) copy-start(s32[4096]{0:T(1024)} %param.15) | copy-start | bytes 49156
  23.0 2.2 %copy-start = (bf16[64,64,512]{2,1,0:T(8,128)(2,1)S(1)}, bf16[64,64,512]{2,1,0:T(8,128)(2,1)}, u32[]{:S(2)}) copy-start(bf16[64,64,512]{2,1,0:T(8,128)(2,1)} %get-tuple-element.9.turned) | copy-start | bytes 12582916

commit v2 on v1

--- a/solution.py
+++ b/solution.py
@@ -12,6 +12,7 @@
 f32 = jnp.float32
 bf16 = jnp.bfloat16
 i32 = jnp.int32
+i16 = jnp.int16
 
 
 def iota(shape, dim):
@@ -30,8 +31,12 @@
     return jnp.where(mask, f32(1.0), f32(0.0)).astype(bf16)
 
 
+def onehot16(left, right):
+    return jnp.where(left == right, bf16(1.0), bf16(0.0))
+
+
 def tiler(width, order):
-    return onehot(lax.rem(iota((width, order), 0), order) == iota((width, order), 1))
+    return onehot((iota((width, order), 0) & (order - 1)) == iota((width, order), 1))
 
 
 def block_diagonal(matrix, width, flipped):
@@ -42,7 +47,8 @@
     else:
         half = nn(spread, matrix)
     full = nt(half.astype(bf16), spread)
-    same = lax.div(iota((width, width), 0), order) == lax.div(iota((width, width), 1), order)
+    bits = order.bit_length() - 1
+    same = (iota((width, width), 0) >> bits) == (iota((width, width), 1) >> bits)
     return jnp.where(same, full, f32(0.0)).astype(bf16)
 
 
@@ -61,26 +67,18 @@
 
 
 def typed_sum(rows, kinds, tables, width, count):
-    wide = jnp.concatenate([kinds] * (width // 128), axis=1)
-    rows = rows.astype(f32)
-    total = None
-    for kind in range(count):
-        part = nn(
-            jnp.where(wide == kind, rows, f32(0.0)).astype(bf16),
-            tables[kind * width : (kind + 1) * width, :],
-        )
-        total = part if total is None else total + part
-    return total
+    wide = jnp.concatenate([kinds.astype(i16)] * (width // 128), axis=1)
+    parts = [jnp.where(wide == i16(kind), rows, bf16(0.0)) for kind in range(count)]
+    return nn(jnp.concatenate(parts, axis=1), tables[...])
 
 
 def restrict_kernel(
-    geometry, fine_ref, owner_ref, slot_ref, kind_ref, table_ref, inverse_ref,
-    local_ref, out_ref, turned_ref, tables, perm, total,
+    geometry, fine_ref, owner_ref, slot_ref, kind_ref, table_ref,
+    local_ref, out_ref, tables, total,
 ):
     coarse, ghost, width, order, kinds, n_py = geometry
     me = lax.axis_index("px") * n_py + lax.axis_index("py")
     step = pl.program_id(0)
-    half = 8 * order
 
     @pl.when(step == 0)
     def _():
@@ -88,10 +86,6 @@
             tables[kind * width : (kind + 1) * width, :] = block_diagonal(
                 table_ref[kind], width, True
             )
-        at = iota((half, half), 0)
-        perm[...] = onehot(
-            iota((half, half), 1) == lax.rem(at, 8) * order + lax.div(at, 8)
-        )
         total[...] = jnp.zeros_like(total)
 
     chunk = fine_ref.shape[0]
@@ -102,13 +96,8 @@
         ).astype(bf16)
         target = target_rows(owner_ref[:, span], slot_ref[:, span], me, coarse, ghost)
         rows = coarse + 4 * ghost
-        total[...] += nn(onehot(iota((rows, 512), 0) == target), contrib)
-
-    halves = [
-        nt(perm[...], inverse_ref[:, at * half : (at + 1) * half]).reshape(order, 8, coarse)
-        for at in range(2)
-    ]
-    turned_ref[...] = jnp.concatenate(halves, axis=1).astype(bf16)
+        picks = onehot16(iota((rows, 512), 0).astype(i16), target.astype(i16))
+        total[...] += nn(picks, contrib)
 
     @pl.when(step == pl.num_programs(0) - 1)
     def _():
@@ -117,9 +106,9 @@
 
 
 def coarse_kernel(
-    geometry, local_ref, outgoing, ghost_row_ref, turned, face_ref, coef_ref, index_ref,
-    neighbour_ref, solution_ref, returned,
-    incoming, reply, xt, first_t, near, code, beside,
+    geometry, local_ref, outgoing, ghost_row_ref, inverse_ref, face_ref, coef_ref, index_ref,
+    neighbour_ref, table_ref, solution_ref, returned, tables_ref,
+    blocks, turned, perm, couplings, block_sem, incoming, reply, xt, first_t, near, code, beside,
     ghost_send, ghost_recv, reply_send, reply_recv, halo_send, halo_recv,
 ):
     coarse, ghost, width, order, n_px, n_py, kinds = geometry
@@ -128,6 +117,8 @@
     px = lax.axis_index("px")
     py = lax.axis_index("py")
     me = px * n_py + py
+    fetch = pltpu.make_async_copy(inverse_ref, blocks, block_sem)
+    fetch.start()
     exists = [py > 0, py < n_py - 1, px > 0, px < n_px - 1]
     place = [(px, py - 1), (px, py + 1), (px - 1, py), (px + 1, py)]
     far = [(py > 1, (px, py - 2)), (py < n_py - 2, (px, py + 2))]
@@ -172,6 +163,11 @@
 
     start_lists(outgoing, incoming, ghost_send, ghost_recv)
 
+    half = 8 * order
+    at = iota((half, half), 0)
+    perm[...] = onehot(iota((half, half), 1) == (at & 7) * order + (at >> 3))
+    for face in range(faces):
+        couplings[face] = block_diagonal(face_ref[face], width, False)
     offset = lax.shift_right_logical(neighbour_ref[...], coarse.bit_length() - 1) - me
     slot = jnp.where(
         offset == 0, 0,
@@ -189,6 +185,21 @@
         == iota((4 * ghost, coarse), 1)
     )
 
+    fetch.wait()
+
+    def turn(group, _):
+        halves = [
+            nt(
+                perm[...], blocks[:, pl.ds(pl.multiple_of((2 * group + at) * half, half), half)]
+            ).reshape(order, 8, coarse)
+            for at in range(2)
+        ]
+        rows = pl.ds(pl.multiple_of(group * 16, 16), 16)
+        turned[:, rows, :] = jnp.concatenate(halves, axis=1).astype(bf16)
+        return 0
+
+    lax.fori_loop(0, order // 16, turn, 0)
+
     finish_lists(outgoing, incoming, ghost_send, ghost_recv)
     rhs_rows = local_ref[...] + nn(lists_onehot, incoming[...])
     xt[...] = jnp.transpose(rhs_rows.astype(bf16).astype(f32))
@@ -264,16 +275,16 @@
         def _():
             upper(tile).start()
 
-    step_rows = 256
+    step_rows = coarse
     steps = faces * coarse // step_rows
 
     def gather(block, begin, end, fresh):
         def body(step, _):
             rows = pl.ds(pl.multiple_of(step * step_rows, step_rows), step_rows)
-            here = code[rows, :] - block * coarse
-            lane = iota((step_rows, 128), 1)
+            here = (code[rows, :] - block * coarse).astype(i16)
+            lane = iota((step_rows, 128), 1).astype(i16)
             picks = jnp.concatenate(
-                [onehot(here == lane + at * 128) for at in range(tiles)], axis=1
+                [onehot16(here - i16(at * 128), lane) for at in range(tiles)], axis=1
             )
             found = nn(picks, near[block])
             if fresh:
@@ -313,9 +324,8 @@
 
     coupled = jnp.zeros((width, coarse), f32)
     for face in range(faces):
-        matrix = block_diagonal(face_ref[face], width, False)
         rows = slice(face * coarse, (face + 1) * coarse)
-        coupled += nt(matrix, beside[rows, :].astype(bf16)) * scales[face : face + 1, :]
+        coupled += nt(couplings[face], beside[rows, :].astype(bf16)) * scales[face : face + 1, :]
     xt[...] = coupled.astype(bf16).astype(f32)
 
     for tile in range(tiles):
@@ -325,6 +335,10 @@
 
     reply[...] = nn(pick_onehot, solution_ref[...].astype(bf16)).astype(bf16)
     start_lists(reply, returned, reply_send, reply_recv)
+    for kind in range(table_ref.shape[0]):
+        tables_ref[kind * width : (kind + 1) * width, :] = block_diagonal(
+            table_ref[kind], width, False
+        )
     for tile in range(tiles):
         to_partner(tile).wait_send()
 
@@ -343,8 +357,8 @@
 
 
 def prolong_kernel(
-    geometry, solution_ref, returned_ref, owner_ref, slot_ref, kind_ref, table_ref,
-    out_solution_ref, fine_ref, tables, held,
+    geometry, solution_ref, returned_ref, owner_ref, slot_ref, kind_ref, tables,
+    out_solution_ref, fine_ref, held,
 ):
     coarse, ghost, width, order, kinds, n_py = geometry
     me = lax.axis_index("px") * n_py + lax.axis_index("py")
@@ -352,18 +366,17 @@
 
     @pl.when(step == 0)
     def _():
-        for kind in range(kinds):
-            tables[kind * width : (kind + 1) * width, :] = block_diagonal(
-                table_ref[kind], width, False
-            )
         held[:coarse, :] = solution_ref[...].astype(bf16)
         held[coarse:, :] = returned_ref[...]
         out_solution_ref[...] = solution_ref[...]
 
     rows = coarse + 4 * ghost
     target = columns_of(target_rows(owner_ref[...], slot_ref[...], me, coarse, ghost))
-    lane = iota(target.shape, 1)
-    picks = jnp.concatenate([onehot(target == lane + at) for at in range(0, rows, 128)], axis=1)
+    target = target.astype(i16)
+    lane = iota(target.shape, 1).astype(i16)
+    picks = jnp.concatenate(
+        [onehot16(target - i16(at), lane) for at in range(0, rows, 128)], axis=1
+    )
     fetched = nn(picks, held[...]).astype(bf16)
     fine_ref[...] = typed_sum(
         fetched, columns_of(kind_ref[...]), tables, width, kinds
@@ -386,50 +399,53 @@
     whole = pl.BlockSpec(memory_space=pltpu.VMEM)
     grant = 48 * 1024 * 1024
 
-    steps = order // 16
-    chunk = fine // steps
+    chunk = 1024
     geometry = (coarse, ghost, width, order, kinds, n_py)
     row = pl.BlockSpec((1, chunk), lambda i: (0, i))
-    local, outgoing, turned = pl.pallas_call(
+    local, outgoing = pl.pallas_call(
         functools.partial(restrict_kernel, geometry),
-        grid=(steps,),
+        grid=(fine // chunk,),
         in_specs=[
             pl.BlockSpec((chunk, width), lambda i: (i, 0)),
             row, row, row,
             pl.BlockSpec((kinds, order, order), lambda i: (0, 0, 0)),
-            pl.BlockSpec((coarse, 16 * order), lambda i: (0, i)),
         ],
         out_specs=[
             pl.BlockSpec((coarse, width), lambda i: (0, 0)),
             pl.BlockSpec((4 * ghost, width), lambda i: (0, 0)),
-            pl.BlockSpec((order, 16, coarse), lambda i: (0, i, 0)),
         ],
         out_shape=[
             jax.ShapeDtypeStruct((coarse, width), f32),
             jax.ShapeDtypeStruct((4 * ghost, width), bf16),
-            jax.ShapeDtypeStruct((order, order, coarse), bf16),
         ],
         scratch_shapes=[
             pltpu.VMEM((kinds * width, width), bf16),
-            pltpu.VMEM((8 * order, 8 * order), bf16),
             pltpu.VMEM((coarse + 4 * ghost, width), f32),
         ],
-        compiler_params=pltpu.CompilerParams(vmem_limit_bytes=grant),
+        compiler_params=pltpu.CompilerParams(vmem_limit_bytes=63400000),
         name="restrict",
-    )(fine_residual, owner, slot, kind, restrict_table, inverse_blocks)
+    )(fine_residual, owner, slot, kind, restrict_table)
 
     tiles = coarse // 128
-    solved, returned = pl.pallas_call(
+    solved, returned, tables = pl.pallas_call(
         functools.partial(
             coarse_kernel, (coarse, ghost, width, order, n_px, n_py, face_coef.shape[0])
         ),
-        in_specs=[whole] * 5 + [pl.BlockSpec(memory_space=pltpu.SMEM)] + [whole] * 2,
-        out_specs=[whole] * 2,
+        in_specs=[whole] * 3
+        + [pl.BlockSpec(memory_space=pl.ANY), whole, pl.BlockSpec(memory_space=pltpu.SMEM)]
+        + [whole] * 3,
+        out_specs=[whole] * 3,
         out_shape=[
             jax.ShapeDtypeStruct((coarse, width), f32),
             jax.ShapeDtypeStruct((4 * ghost, width), bf16),
+            jax.ShapeDtypeStruct((kinds * width, width), bf16),
         ],
         scratch_shapes=[
+            pltpu.VMEM(inverse_blocks.shape, bf16),
+            pltpu.VMEM((order, order, coarse), bf16),
+            pltpu.VMEM((8 * order, 8 * order), bf16),
+            pltpu.VMEM((faces, width, width), bf16),
+            pltpu.SemaphoreType.DMA,
             pltpu.VMEM((4 * ghost, width), bf16),
             pltpu.VMEM((4 * ghost, width), bf16),
             pltpu.VMEM((width, coarse), f32),
@@ -445,8 +461,8 @@
         ),
         name="coarse",
     )(
-        local, outgoing, ghost_slot.reshape(1, 4 * ghost), turned, face_table,
-        face_coef.reshape(1, -1), coef_index, neighbours,
+        local, outgoing, ghost_slot.reshape(1, 4 * ghost), inverse_blocks, face_table,
+        face_coef.reshape(1, -1), coef_index, neighbours, restrict_table,
     )
 
     chunk = 512
@@ -458,7 +474,7 @@
             pl.BlockSpec((coarse, width), lambda i: (0, 0)),
             pl.BlockSpec((4 * ghost, width), lambda i: (0, 0)),
             row, row, row,
-            pl.BlockSpec((kinds, order, order), lambda i: (0, 0, 0)),
+            pl.BlockSpec((kinds * width, width), lambda i: (0, 0)),
         ],
         out_specs=[
             pl.BlockSpec((coarse, width), lambda i: (0, 0)),
@@ -469,12 +485,11 @@
             jax.ShapeDtypeStruct((fine, width), bf16),
         ],
         scratch_shapes=[
-            pltpu.VMEM((kinds * width, width), bf16),
             pltpu.VMEM((coarse + 4 * ghost, width), bf16),
         ],
         compiler_params=pltpu.CompilerParams(vmem_limit_bytes=grant),
         name="prolong",
-    )(solved, returned, owner, slot, kind, restrict_table)
+    )(solved, returned, owner, slot, kind, tables)
 
 
 def solution(mesh):

time: 75.4 us -> 57.2 us (0.76)
  Pallas kernels: 66.6 us -> 53.5 us
  local copies, waits for them, and re-layouts: 7.63 us -> 2.76 us
    pallas_call x1, Pallas kernels: 16.9 us -> 9.91 us  [shards(): pl.pallas_call(functools.partial(restrict_kernel, geometry), grid=(fine /...]
    pallas_call x1, Pallas kernels: 36.6 us -> 31.4 us  [shards(): pl.pallas_call(functools.partial(coarse_kernel, (coarse, ghost, width, or...]
    unnamed x28 -> x20, local copies, waits for them, and re-layouts: 6.86 us -> 1.91 us
    pallas_call x1, Pallas kernels: 13.1 us -> 12.2 us  [shards(): pl.pallas_call(functools.partial(prolong_kernel, geometry), grid=(fine //...]
where the time goes in v2:
time: 57.2 us; the launch traced here: 57 us
  Pallas kernels  53.5 us (94%)
  local copies, waits for them, and re-layouts  2.76 us (5%)
  between operations  0.74 us (1%)
    pallas_call x1, Pallas kernels, shards(): pl.pallas_call(functools.partial(coarse_kernel, (coarse, ghost, width, or...  31.4 us
    pallas_call x1, Pallas kernels, shards(): pl.pallas_call(functools.partial(prolong_kernel, geometry), grid=(fine //...  12.2 us
    pallas_call x1, Pallas kernels, shards(): pl.pallas_call(functools.partial(restrict_kernel, geometry), grid=(fine /...  9.91 us
    unnamed x20, local copies, waits for them, and re-layouts  1.91 us

profile of v2, /device:TPU:0, one launch (start us, length us, event | category | flops | bytes accessed | tf_op | source)
XLA Modules:
  0.0 57.0 jit_solution(13540892504542684551)
XLA Ops:
  0.6 0.0 copy-start
  0.6 0.0 copy-start.8
  0.7 0.0 copy-start.7
  0.7 0.0 copy-start.9
  0.7 0.0 copy-start.2
  0.7 0.8 %reshape.22.ghost_row_ref = s32[1,128]{1,0:T(1,128)S(1)} reshape(s32[4,32]{1,0:T(4,128)} %param.14) | data formatting | bytes 1024 | tf_op jit(solution)/shard_map/reshape | solution.py:464
  1.5 9.9 %restrict.1 = (f32[512,256]{1,0:T(8,128)}, bf16[128,256]{1,0:T(8,128)(2,1)}) custom-call(bf16[4096,256]{1,0:T(8,128)(2,1)} %fine_ref.1, s32[1,4096]{1,0:T(1,128)} %bitcast.4, s32[1,4096]{1,0:T(1,128)} %bitcast.6, s32[1,4096]{1,0:T(1,128)} %bitcast.8, bf16[8,64,64]{2,1,0:T(8,128)(2,1)} %table_ref.3), custom_call_target="tpu_custom_call" | custom-call | tf_op jit(solution)/shard_map/restrict/pallas_call | solution.py:405
  11.4 0.0 copy-done
  11.4 0.0 copy-done.8
  11.4 0.0 copy-done.7
  11.5 0.0 copy-done.9
  11.5 0.0 copy-done.2
  11.5 0.0 copy-start.1
  11.5 1.0 %copy-done.1 = f32[512,256]{1,0:T(8,128)S(1)} copy-done((f32[512,256]{1,0:T(8,128)S(1)}, f32[512,256]{1,0:T(8,128)}, u32[]{:S(2)}) %copy-start.1) | copy-done | bytes 524312
  12.5 0.0 copy-start.3
  12.5 0.8 %copy-done.3 = bf16[128,256]{1,0:T(8,128)(2,1)S(1)} copy-done((bf16[128,256]{1,0:T(8,128)(2,1)S(1)}, bf16[128,256]{1,0:T(8,128)(2,1)}, u32[]{:S(2)}) %copy-start.3) | copy-done | bytes 65560
  13.4 0.0 copy-start.4
  13.4 0.0 copy-start.5
  13.4 0.0 copy-start.6
  13.4 31.4 %coarse.1 = (f32[512,256]{1,0:T(8,128)S(1)}, bf16[128,256]{1,0:T(8,128)(2,1)S(1)}, bf16[2048,256]{1,0:T(8,128)(2,1)S(1)}) custom-call(f32[512,256]{1,0:T(8,128)S(1)} %copy-done.1, bf16[128,256]{1,0:T(8,128)(2,1)S(1)} %copy-done.3, s32[1,128]{1,0:T(1,128)S(1)} %reshape.22.ghost_row_ref, bf16[512,4096]{1,0:T(8,128)(2,1)} %inverse_ref.1, ...), custom_call_target="tpu_custom_call" | custom-call | tf_op jit(solution)/shard_map/coarse/pallas_call | solution.py:430
  44.7 0.0 copy-done.4
  44.7 0.0 copy-done.5
  44.8 0.0 copy-done.6
  44.8 12.2 %prolong.1 = (f32[512,256]{1,0:T(8,128)}, bf16[4096,256]{1,0:T(8,128)(2,1)}) custom-call(f32[512,256]{1,0:T(8,128)S(1)} %get-tuple-element.9.solution_ref, bf16[128,256]{1,0:T(8,128)(2,1)S(1)} %get-tuple-element.10.returned_ref, s32[1,4096]{1,0:T(1,128)S(1)} %bitcast.5, s32[1,4096]{1,0:T(1,128)S(1)} %bitcast.7, s32[1,4096]{1,0:T(1,128)S(1)} %bitcast.9, ...), custom_call_target="tpu_custom_call" | custom-call | tf_op jit(solution)/shard_map/prolong/pallas_call | solution.py:470
Async XLA Ops:
  0.6 10.8 %copy-start = (bf16[8,64,64]{2,1,0:T(8,128)(2,1)S(1)}, bf16[8,64,64]{2,1,0:T(8,128)(2,1)}, u32[]{:S(2)}) copy-start(bf16[8,64,64]{2,1,0:T(8,128)(2,1)} %table_ref.3) | copy-start | bytes 196612
  0.6 10.8 %copy-start.8 = (s32[6,512]{1,0:T(8,128)S(1)}, s32[6,512]{1,0:T(8,128)}, u32[]{:S(2)}) copy-start(s32[6,512]{1,0:T(8,128)} %neighbour_ref.1) | copy-start | bytes 36868
  0.7 10.8 %copy-start.7 = (s32[6,512]{1,0:T(8,128)S(1)}, s32[6,512]{1,0:T(8,128)}, u32[]{:S(2)}) copy-start(s32[6,512]{1,0:T(8,128)} %index_ref.1) | copy-start | bytes 36868
  0.7 10.8 %copy-start.9 = (f32[16]{0:T(128)S(1)}, f32[16]{0:T(128)}, u32[]{:S(2)}) copy-start(f32[16]{0:T(128)} %param.19) | copy-start | bytes 196
  0.7 10.8 %copy-start.2 = (bf16[6,64,64]{2,1,0:T(8,128)(2,1)S(1)}, bf16[6,64,64]{2,1,0:T(8,128)(2,1)}, u32[]{:S(2)}) copy-start(bf16[6,64,64]{2,1,0:T(8,128)(2,1)} %face_ref.1) | copy-start | bytes 147460
  11.5 1.0 %copy-start.1 = (f32[512,256]{1,0:T(8,128)S(1)}, f32[512,256]{1,0:T(8,128)}, u32[]{:S(2)}) copy-start(f32[512,256]{1,0:T(8,128)} %get-tuple-element.7.local_ref) | copy-start | bytes 1572868
  12.5 0.8 %copy-start.3 = (bf16[128,256]{1,0:T(8,128)(2,1)S(1)}, bf16[128,256]{1,0:T(8,128)(2,1)}, u32[]{:S(2)}) copy-start(bf16[128,256]{1,0:T(8,128)(2,1)} %get-tuple-element.8.outgoing) | copy-start | bytes 196612
  13.4 31.4 %copy-start.4 = (s32[4096]{0:T(1024)S(1)}, s32[4096]{0:T(1024)}, u32[]{:S(2)}) copy-start(s32[4096]{0:T(1024)} %param.12) | copy-start | bytes 49156
  13.4 31.4 %copy-start.5 = (s32[4096]{0:T(1024)S(1)}, s32[4096]{0:T(1024)}, u32[]{:S(2)}) copy-start(s32[4096]{0:T(1024)} %param.13) | copy-start | bytes 49156
  13.4 31.4 %copy-start.6 = (s32[4096]{0:T(1024)S(1)}, s32[4096]{0:T(1024)}, u32[]{:S(2)}) copy-start(s32[4096]{0:T(1024)} %param.15) | copy-start | bytes 49156

commit v3 on v2

--- a/solution.py
+++ b/solution.py
@@ -106,9 +106,9 @@
 
 
 def coarse_kernel(
-    geometry, local_ref, outgoing, ghost_row_ref, inverse_ref, face_ref, coef_ref, index_ref,
+    geometry, sums_ref, outgoing, ghost_ref, inverse_ref, face_ref, coef_ref, index_ref,
     neighbour_ref, table_ref, solution_ref, returned, tables_ref,
-    blocks, turned, perm, couplings, block_sem, incoming, reply, xt, first_t, near, code, beside,
+    blocks, local_ref, turned, perm, couplings, block_sem, sums_sem, incoming, reply, xt, first_t, near, code, beside,
     ghost_send, ghost_recv, reply_send, reply_recv, halo_send, halo_recv,
 ):
     coarse, ghost, width, order, n_px, n_py, kinds = geometry
@@ -119,6 +119,8 @@
     me = px * n_py + py
     fetch = pltpu.make_async_copy(inverse_ref, blocks, block_sem)
     fetch.start()
+    fetch_sums = pltpu.make_async_copy(sums_ref, local_ref, sums_sem)
+    fetch_sums.start()
     exists = [py > 0, py < n_py - 1, px > 0, px < n_px - 1]
     place = [(px, py - 1), (px, py + 1), (px - 1, py), (px + 1, py)]
     far = [(py > 1, (px, py - 2)), (py < n_py - 2, (px, py + 2))]
@@ -175,17 +177,21 @@
     )
     codes = slot * coarse + (neighbour_ref[...] & (coarse - 1))
     for face in range(faces):
-        code[face * coarse : (face + 1) * coarse, :] = columns_of(codes[face : face + 1, :])
+        code[face * coarse : (face + 1) * coarse, :] = columns_of(
+            codes[face : face + 1, :]
+        ).astype(i16)
     scales = jnp.zeros(index_ref.shape, f32)
     for kind in range(kinds):
         scales = jnp.where(index_ref[...] == kind, coef_ref[0, kind], scales)
-    lists_onehot = onehot(iota((coarse, 4 * ghost), 0) == ghost_row_ref[...])
+    ghost_row = jnp.concatenate([ghost_ref[at : at + 1, :] for at in range(4)], axis=1)
+    lists_onehot = onehot(iota((coarse, 4 * ghost), 0) == ghost_row)
     pick_onehot = onehot(
-        jnp.concatenate([columns_of(ghost_row_ref[...])] * (coarse // 128), axis=1)
+        jnp.concatenate([columns_of(ghost_row)] * (coarse // 128), axis=1)
         == iota((4 * ghost, coarse), 1)
     )
 
     fetch.wait()
+    fetch_sums.wait()
 
     def turn(group, _):
         halves = [
@@ -275,25 +281,25 @@
         def _():
             upper(tile).start()
 
-    step_rows = coarse
-    steps = faces * coarse // step_rows
-
-    def gather(block, begin, end, fresh):
-        def body(step, _):
-            rows = pl.ds(pl.multiple_of(step * step_rows, step_rows), step_rows)
-            here = (code[rows, :] - block * coarse).astype(i16)
-            lane = iota((step_rows, 128), 1).astype(i16)
-            picks = jnp.concatenate(
-                [onehot16(here - i16(at * 128), lane) for at in range(tiles)], axis=1
-            )
-            found = nn(picks, near[block])
-            if fresh:
-                beside[rows, :] = found
-            else:
-                beside[rows, :] += found
-            return 0
-
-        lax.fori_loop(begin, end, body, 0)
+    def picked(face, block):
+        rows = pl.ds(pl.multiple_of(face * coarse, coarse), coarse)
+        here = code[rows, :] - jnp.asarray(block * coarse, i32).astype(i16)
+        lane = iota((coarse, 128), 1).astype(i16)
+        picks = jnp.concatenate(
+            [onehot16(here - i16(at * 128), lane) for at in range(tiles)], axis=1
+        )
+        return nn(picks, near[block])
+
+    def own_pass(face, _):
+        rows = pl.ds(pl.multiple_of(face * coarse, coarse), coarse)
+        beside[rows, :] = picked(face, 0).astype(bf16)
+        return 0
+
+    def middle_pass(face, _):
+        rows = pl.ds(pl.multiple_of(face * coarse, coarse), coarse)
+        found = picked(face, 3) + picked(face, 4) + picked(face, partner)
+        beside[rows, :] += found.astype(bf16)
+        return 0
 
     for tile in range(tiles):
         from_partner(tile).wait_recv()
@@ -301,31 +307,29 @@
         @pl.when(relays)
         def _():
             onward(tile).start()
-        gather(0, tile * steps // tiles, (tile + 1) * steps // tiles, True)
-    gather(partner, 0, steps, False)
+        lax.fori_loop(tile * faces // tiles, (tile + 1) * faces // tiles, own_pass, 0)
 
     @pl.when(exists[2])
     def _():
         for tile in range(tiles):
             halo(3, tile, 0, 3, place[2]).wait_recv()
-    gather(3, 0, steps, False)
 
     @pl.when(exists[3])
     def _():
         for tile in range(tiles):
             halo(2, tile, 0, 4, place[3]).wait_recv()
-    gather(4, 0, steps, False)
+    lax.fori_loop(0, faces, middle_pass, 0)
 
     @pl.when(gets_relay)
     def _():
         for tile in range(tiles):
             from_relay(tile).wait_recv()
-    gather(beyond, 0, steps, False)
 
     coupled = jnp.zeros((width, coarse), f32)
     for face in range(faces):
         rows = slice(face * coarse, (face + 1) * coarse)
-        coupled += nt(couplings[face], beside[rows, :].astype(bf16)) * scales[face : face + 1, :]
+        found = beside[rows, :] + picked(face, beyond).astype(bf16)
+        coupled += nt(couplings[face], found) * scales[face : face + 1, :]
     xt[...] = coupled.astype(bf16).astype(f32)
 
     for tile in range(tiles):
@@ -371,16 +375,19 @@
         out_solution_ref[...] = solution_ref[...]
 
     rows = coarse + 4 * ghost
-    target = columns_of(target_rows(owner_ref[...], slot_ref[...], me, coarse, ghost))
-    target = target.astype(i16)
-    lane = iota(target.shape, 1).astype(i16)
-    picks = jnp.concatenate(
-        [onehot16(target - i16(at), lane) for at in range(0, rows, 128)], axis=1
-    )
-    fetched = nn(picks, held[...]).astype(bf16)
-    fine_ref[...] = typed_sum(
-        fetched, columns_of(kind_ref[...]), tables, width, kinds
-    ).astype(bf16)
+    for begin in range(0, fine_ref.shape[0], 512):
+        span = slice(begin, begin + 512)
+        target = columns_of(
+            target_rows(owner_ref[:, span], slot_ref[:, span], me, coarse, ghost)
+        ).astype(i16)
+        lane = iota(target.shape, 1).astype(i16)
+        picks = jnp.concatenate(
+            [onehot16(target - i16(at), lane) for at in range(0, rows, 128)], axis=1
+        )
+        fetched = nn(picks, held[...]).astype(bf16)
+        fine_ref[span, :] = typed_sum(
+            fetched, columns_of(kind_ref[:, span]), tables, width, kinds
+        ).astype(bf16)
 
 
 def shards(
@@ -431,8 +438,8 @@
         functools.partial(
             coarse_kernel, (coarse, ghost, width, order, n_px, n_py, face_coef.shape[0])
         ),
-        in_specs=[whole] * 3
-        + [pl.BlockSpec(memory_space=pl.ANY), whole, pl.BlockSpec(memory_space=pltpu.SMEM)]
+        in_specs=[pl.BlockSpec(memory_space=pltpu.HBM)] * 2
+        + [whole, pl.BlockSpec(memory_space=pltpu.HBM), whole, pl.BlockSpec(memory_space=pltpu.SMEM)]
         + [whole] * 3,
         out_specs=[whole] * 3,
         out_shape=[
@@ -442,17 +449,19 @@
         ],
         scratch_shapes=[
             pltpu.VMEM(inverse_blocks.shape, bf16),
+            pltpu.VMEM((coarse, width), f32),
             pltpu.VMEM((order, order, coarse), bf16),
             pltpu.VMEM((8 * order, 8 * order), bf16),
             pltpu.VMEM((faces, width, width), bf16),
+            pltpu.SemaphoreType.DMA,
             pltpu.SemaphoreType.DMA,
             pltpu.VMEM((4 * ghost, width), bf16),
             pltpu.VMEM((4 * ghost, width), bf16),
             pltpu.VMEM((width, coarse), f32),
             pltpu.VMEM((width, coarse), f32),
             pltpu.VMEM((5, coarse, width), bf16),
-            pltpu.VMEM((faces * coarse, 128), i32),
-            pltpu.VMEM((faces * coarse, width), f32),
+            pltpu.VMEM((faces * coarse, 128), i16),
+            pltpu.VMEM((faces * coarse, width), bf16),
         ]
         + [pltpu.SemaphoreType.DMA((4,))] * 4
         + [pltpu.SemaphoreType.DMA((4, tiles))] * 2,
@@ -461,11 +470,11 @@
         ),
         name="coarse",
     )(
-        local, outgoing, ghost_slot.reshape(1, 4 * ghost), inverse_blocks, face_table,
+        local, outgoing, ghost_slot, inverse_blocks, face_table,
         face_coef.reshape(1, -1), coef_index, neighbours, restrict_table,
     )
 
-    chunk = 512
+    chunk = 1024
     row = pl.BlockSpec((1, chunk), lambda i: (0, i))
     return pl.pallas_call(
         functools.partial(prolong_kernel, geometry),

time: 57.2 us -> 50.7 us (0.89)
  Pallas kernels: 53.5 us -> 47.8 us
  local copies, waits for them, and re-layouts: 2.76 us -> 1.91 us
    pallas_call x1, Pallas kernels: 12.2 us -> 7.97 us  [shards(): pl.pallas_call(functools.partial(prolong_kernel, geometry), grid=(fine //...]
    pallas_call x1, Pallas kernels: 31.4 us -> 29.9 us  [shards(): pl.pallas_call(functools.partial(coarse_kernel, (coarse, ghost, width, or...]
    reshape x1 -> x0, local copies, waits for them, and re-layouts: 0.85 us -> none  [shards(): ghost_slot.reshape(1, 4 * ghost)]
    unnamed x20 -> x22, local copies, waits for them, and re-layouts: 1.91 us -> 1.91 us
where the time goes in v3:
time: 50.7 us; the launch traced here: 50.5 us
  Pallas kernels  47.8 us (94%)
  local copies, waits for them, and re-layouts  1.91 us (4%)
  between operations  0.76 us (1%)
    pallas_call x1, Pallas kernels, shards(): pl.pallas_call(functools.partial(coarse_kernel, (coarse, ghost, width, or...  29.9 us
    pallas_call x1, Pallas kernels, shards(): pl.pallas_call(functools.partial(restrict_kernel, geometry), grid=(fine /...  10 us
    pallas_call x1, Pallas kernels, shards(): pl.pallas_call(functools.partial(prolong_kernel, geometry), grid=(fine //...  7.97 us
    unnamed x22, local copies, waits for them, and re-layouts  1.91 us

profile of v3, /device:TPU:0, one launch (start us, length us, event | category | flops | bytes accessed | tf_op | source)
XLA Modules:
  0.0 50.5 jit_solution(6582345566902073171)
XLA Ops:
  0.6 0.0 copy-start.1
  0.6 0.0 copy-start.8
  0.7 0.0 copy-start.7
  0.7 0.0 copy-start.10
  0.7 0.0 copy-start.2
  0.7 0.0 copy-start.9
  0.7 10.0 %restrict.1 = (f32[512,256]{1,0:T(8,128)}, bf16[128,256]{1,0:T(8,128)(2,1)}) custom-call(bf16[4096,256]{1,0:T(8,128)(2,1)} %fine_ref.1, s32[1,4096]{1,0:T(1,128)} %bitcast.4, s32[1,4096]{1,0:T(1,128)} %bitcast.6, s32[1,4096]{1,0:T(1,128)} %bitcast.8, bf16[8,64,64]{2,1,0:T(8,128)(2,1)} %table_ref.3), custom_call_target="tpu_custom_call" | custom-call | tf_op jit(solution)/shard_map/restrict/pallas_call | solution.py:412
  10.7 0.0 copy-done.1
  10.7 0.0 copy-done.8
  10.7 0.0 copy-done.7
  10.7 0.0 copy-done.10
  10.7 0.0 copy-done.2
  10.7 0.0 copy-done.9
  10.8 0.0 copy-start
  10.8 1.0 %copy-done = f32[512,256]{1,0:T(8,128)S(1)} copy-done((f32[512,256]{1,0:T(8,128)S(1)}, f32[512,256]{1,0:T(8,128)}, u32[]{:S(2)}) %copy-start) | copy-done | bytes 524312
  11.8 0.0 copy-start.3
  11.8 0.8 %copy-done.3 = bf16[128,256]{1,0:T(8,128)(2,1)S(1)} copy-done((bf16[128,256]{1,0:T(8,128)(2,1)S(1)}, bf16[128,256]{1,0:T(8,128)(2,1)}, u32[]{:S(2)}) %copy-start.3) | copy-done | bytes 65560
  12.6 0.0 copy-start.4
  12.6 0.0 copy-start.5
  12.6 0.0 copy-start.6
  12.6 29.9 %coarse.1 = (f32[512,256]{1,0:T(8,128)S(1)}, bf16[128,256]{1,0:T(8,128)(2,1)S(1)}, bf16[2048,256]{1,0:T(8,128)(2,1)S(1)}) custom-call(f32[512,256]{1,0:T(8,128)S(1)} %copy-done, bf16[128,256]{1,0:T(8,128)(2,1)S(1)} %copy-done.3, s32[4,32]{1,0:T(4,128)S(1)} %copy-done.9, bf16[512,4096]{1,0:T(8,128)(2,1)} %inverse_ref.1, bf16[6,64,64]{2,1,0:T(8,128)(2,1)S(1)} %copy-done.2, ...), custom_call_target="tpu_custom_call" | custom-call | tf_op jit(solution)/shard_map/coarse/pallas_call | solution.py:437
  42.5 0.0 copy-done.4
  42.5 0.0 copy-done.5
  42.5 0.0 copy-done.6
  42.5 8.0 %prolong.1 = (f32[512,256]{1,0:T(8,128)}, bf16[4096,256]{1,0:T(8,128)(2,1)}) custom-call(f32[512,256]{1,0:T(8,128)S(1)} %get-tuple-element.9.solution_ref, bf16[128,256]{1,0:T(8,128)(2,1)S(1)} %get-tuple-element.10.returned_ref, s32[1,4096]{1,0:T(1,128)S(1)} %bitcast.5, s32[1,4096]{1,0:T(1,128)S(1)} %bitcast.7, s32[1,4096]{1,0:T(1,128)S(1)} %bitcast.9, ...), custom_call_target="tpu_custom_call" | custom-call | tf_op jit(solution)/shard_map/prolong/pallas_call | solution.py:479
Async XLA Ops:
  0.6 10.1 %copy-start.1 = (bf16[8,64,64]{2,1,0:T(8,128)(2,1)S(1)}, bf16[8,64,64]{2,1,0:T(8,128)(2,1)}, u32[]{:S(2)}) copy-start(bf16[8,64,64]{2,1,0:T(8,128)(2,1)} %table_ref.3) | copy-start | bytes 196612
  0.6 10.1 %copy-start.8 = (s32[6,512]{1,0:T(8,128)S(1)}, s32[6,512]{1,0:T(8,128)}, u32[]{:S(2)}) copy-start(s32[6,512]{1,0:T(8,128)} %neighbour_ref.1) | copy-start | bytes 36868
  0.7 10.1 %copy-start.7 = (s32[6,512]{1,0:T(8,128)S(1)}, s32[6,512]{1,0:T(8,128)}, u32[]{:S(2)}) copy-start(s32[6,512]{1,0:T(8,128)} %index_ref.1) | copy-start | bytes 36868
  0.7 10.1 %copy-start.10 = (f32[16]{0:T(128)S(1)}, f32[16]{0:T(128)}, u32[]{:S(2)}) copy-start(f32[16]{0:T(128)} %param.19) | copy-start | bytes 196
  0.7 10.1 %copy-start.2 = (bf16[6,64,64]{2,1,0:T(8,128)(2,1)S(1)}, bf16[6,64,64]{2,1,0:T(8,128)(2,1)}, u32[]{:S(2)}) copy-start(bf16[6,64,64]{2,1,0:T(8,128)(2,1)} %face_ref.1) | copy-start | bytes 147460
  0.7 10.1 %copy-start.9 = (s32[4,32]{1,0:T(4,128)S(1)}, s32[4,32]{1,0:T(4,128)}, u32[]{:S(2)}) copy-start(s32[4,32]{1,0:T(4,128)} %ghost_ref.1) | copy-start | bytes 1540
  10.8 1.0 %copy-start = (f32[512,256]{1,0:T(8,128)S(1)}, f32[512,256]{1,0:T(8,128)}, u32[]{:S(2)}) copy-start(f32[512,256]{1,0:T(8,128)} %get-tuple-element.7.sums_ref) | copy-start | bytes 1572868
  11.8 0.8 %copy-start.3 = (bf16[128,256]{1,0:T(8,128)(2,1)S(1)}, bf16[128,256]{1,0:T(8,128)(2,1)}, u32[]{:S(2)}) copy-start(bf16[128,256]{1,0:T(8,128)(2,1)} %get-tuple-element.8.outgoing) | copy-start | bytes 196612
  12.6 29.9 %copy-start.4 = (s32[4096]{0:T(1024)S(1)}, s32[4096]{0:T(1024)}, u32[]{:S(2)}) copy-start(s32[4096]{0:T(1024)} %param.12) | copy-start | bytes 49156
  12.6 29.9 %copy-start.5 = (s32[4096]{0:T(1024)S(1)}, s32[4096]{0:T(1024)}, u32[]{:S(2)}) copy-start(s32[4096]{0:T(1024)} %param.13) | copy-start | bytes 49156
  12.6 29.9 %copy-start.6 = (s32[4096]{0:T(1024)S(1)}, s32[4096]{0:T(1024)}, u32[]{:S(2)}) copy-start(s32[4096]{0:T(1024)} %param.15) | copy-start | bytes 49156
